TPU v7x, 256 devices: a whole 4x4x8 slice. The times are simulated.
256 devices in a mesh: side: 2 (over core), gx: 16 (over z, x_lo), gy: 8 (over y, x_hi).
Axes of the slice: x: 4 (x_hi: 2, x_lo: 2; x = x_hi * 2 + x_lo), y: 4, z: 8, core: 2. Of those that a mesh axis runs over, the one named last changes fastest.
Arguments:
- fields: float32 [2, 3, 16, 256, 2048], P('side', None, None, 'gx', 'gy'), may hold values from -6 to 6
- source: float32 [2, 3, 16, 256, 2048], P('side', None, None, 'gx', 'gy'), may hold values from -12 to 12
- reaction: float32 [2, 16, 256, 2048], P('side', None, 'gx', 'gy'), may hold values from 0.25 to 4
- velocity: float32 [2, 16, 256, 2048], P('side', None, 'gx', 'gy'), may hold values from 0.5 to 6
- coupling: float32 [2, 3, 3], P('side'), may hold values from -0.5 to 0.5
Outputs:
- new_fields: float32 [2, 3, 16, 256, 2048], P('side', None, None, 'gx', 'gy')
- interface: float32 [2, 3, 256, 2048], P('side', None, 'gx', 'gy')
All inputs are finite; a program needn't handle non-finite values.
Results may differ from a plain program's by a relative error of at most 0.00002.
Values sent between devices are 32-bit elements; how exact they have to be, the bound alone decides.
A program may use at most 64 MiB of HBM per device.

v0:
```python
import jax
import jax.numpy as jnp
from jax import lax
from jax.sharding import PartitionSpec as P

SWEEPS = 4


OMEGA = 0.8
RATIO = 0.5
THETA = 0.7


def from_partner(value, axis, apart):
    mask = 2**apart
    pairs = [(source, source ^ mask) for source in range(lax.axis_size(axis))]
    return lax.ppermute(value, axis, pairs)


def shifted(block, axis, distance):
    devices = range(lax.axis_size(axis))
    route = [((i - distance) % len(devices), i) for i in devices]
    return lax.ppermute(block, axis, route)


def passed_along(value, axis, steps):
    count = lax.axis_size(axis)
    first, last = (max(0, -steps), min(count, count - steps))
    return lax.ppermute(value, axis, [(source, source + steps) for source in range(first, last)])


def relax(
    center,
    west_cells,
    east_cells,
    south_cells,
    north_cells,
    source,
    reaction,
    velocity,
    coupling,
    ghost_layer,
):
    zero_layer = jnp.zeros_like(center[:, :1])
    below = jnp.concatenate([ghost_layer[:, None], center[:, :-1]], axis=1)
    above = jnp.concatenate([center[:, 1:], zero_layer], axis=1)
    beside_all = below + above + west_cells + east_cells + south_cells + north_cells
    diag_term = 6.0 + reaction + velocity
    mixing = jnp.zeros_like(center)
    for index in range(center.shape[0]):
        mixing = mixing + coupling[:, index][:, None, None, None] * center[index][None]
    residual = source - (
        diag_term[None] * center - beside_all - velocity[None] * west_cells + mixing
    )
    scale = diag_term[None] + jnp.diagonal(coupling)[:, None, None, None]
    return center + OMEGA * residual / scale


def trade(layers):
    return from_partner(layers, "side", 0)


def local(fields, source, reaction, velocity, coupling):
    current = fields[0]
    forcing = source[0]
    rates = reaction[0]
    speeds = velocity[0]
    mix_matrix = coupling[0]
    fluid_flag = lax.axis_index("side") == 0
    depth = SWEEPS
    facing = trade(current[:, 0:2])
    for step in range(depth):
        ghost_layer = jnp.where(
            fluid_flag, facing[:, 0], current[:, 0] + RATIO * (facing[:, 1] - facing[:, 0])
        )
        from_west = shifted(current[:, :, -1:], "gx", 1)
        from_east = shifted(current[:, :, :1], "gx", -1)
        from_south = passed_along(current[..., -1:], "gy", 1)
        from_north = passed_along(current[..., :1], "gy", -1)
        west_cells = jnp.concatenate([from_west, current[:, :, :-1]], axis=2)
        east_cells = jnp.concatenate([current[:, :, 1:], from_east], axis=2)
        south_cells = jnp.concatenate([from_south, current[..., :-1]], axis=3)
        north_cells = jnp.concatenate([current[..., 1:], from_north], axis=3)
        current = relax(
            current,
            west_cells,
            east_cells,
            south_cells,
            north_cells,
            forcing,
            rates,
            speeds,
            mix_matrix,
            ghost_layer,
        )
    edge_layer = current[:, 0]
    other_edge = from_partner(edge_layer, "side", 0)
    membrane_trace = jnp.where(fluid_flag, other_edge, edge_layer)
    fluid_trace = jnp.where(fluid_flag, edge_layer, other_edge)
    interface = THETA * membrane_trace + (1.0 - THETA) * fluid_trace
    return (current[None], interface[None])


def solution(mesh):
    placed = (
        P("side", None, None, "gx", "gy"),
        P("side", None, None, "gx", "gy"),
        P("side", None, "gx", "gy"),
        P("side", None, "gx", "gy"),
        P("side", None, None),
    )
    return jax.shard_map(
        local,
        mesh=mesh,
        in_specs=placed,
        out_specs=(P("side", None, None, "gx", "gy"), P("side", None, "gx", "gy")),
        check_vma=False,
    )
```

profile of v0, /device:TPU:29, one launch (start us, length us, event | category | flops | bytes accessed | tf_op | source)
XLA Modules:
  0.0 120.4 jit_solution(3153391488305820479)
XLA Ops:
  0.6 1.8 %fusion.62 = (f32[3,16,1,256]{3,2,1,0:T(1,128)}, f32[3,16,1,256]{3,2,1,0:T(1,128)}) fusion(f32[3,16,16,256]{3,2,1,0:T(8,128)} %bitcast.48), kind=kLoop, calls=%fused_computation.99 | loop fusion | bytes 196608 | tf_op jit(solution)/shard_map/slice | solution.py:76
  2.5 0.9 collective-permute-start.1
  3.4 5.3 %collective-permute-start.2 = (f32[3,16,1,256]{3,2,1,0:T(1,128)}, f32[3,16,1,256]{3,2,1,0:T(1,128)}, u32[]{:S(2)}, u32[]{:S(2)}) collective-permute-start(f32[3,16,1,256]{3,2,1,0:T(1,128)} %get-tuple-element.52), channel_id=1, source_target_pairs={{8,0},{16,8},{24,16},{32,24},{40,32},{48,40},{56,48},{64,56},{72,6... | collective-permute-start | bytes 147464 | tf_op jit(solution)/shard_map/ppermute | solution.py:23
  8.7 1.5 %slice.276 = f32[3,2,16,256]{3,2,1,0:T(8,128)} slice(f32[3,16,16,256]{3,2,1,0:T(8,128)} %bitcast.49), slice={[0:3], [0:2], [0:16], [0:256]} | slice | bytes 196608 | tf_op jit(solution)/shard_map/slice | solution.py:71
  10.2 1.0 collective-permute-start
  11.2 2.1 %fusion.65 = (f32[3,16,16,1]{3,2,1,0:T(8,128)}, f32[3,16,16,1]{3,2,1,0:T(8,128)}) fusion(f32[3,16,16,256]{3,2,1,0:T(8,128)} %bitcast.50), kind=kLoop, calls=%fused_computation.102 | loop fusion | bytes 12288 | tf_op jit(solution)/shard_map/slice | solution.py:79
  13.3 3.2 %collective-permute-start.4 = (f32[3,16,16,1]{3,2,1,0:T(8,128)}, f32[3,16,16,1]{3,2,1,0:T(8,128)}, u32[]{:S(2)}, u32[]{:S(2)}) collective-permute-start(f32[3,16,16,1]{3,2,1,0:T(8,128)} %get-tuple-element.57), channel_id=1, source_target_pairs={{1,0},{2,1},{3,2},{4,3},{5,4},{6,5},{7,6},{9,8},{10,9},{11,10},{12... | collective-permute-start | bytes 9224 | tf_op jit(solution)/shard_map/ppermute | solution.py:29
  16.4 1.3 %collective-permute-start.3 = (f32[3,16,16,1]{3,2,1,0:T(8,128)}, f32[3,16,16,1]{3,2,1,0:T(8,128)}, u32[]{:S(2)}, u32[]{:S(2)}) collective-permute-start(f32[3,16,16,1]{3,2,1,0:T(8,128)} %get-tuple-element.58), channel_id=1, source_target_pairs={{0,1},{1,2},{2,3},{3,4},{4,5},{5,6},{6,7},{8,9},{9,10},{10,11},{11... | collective-permute-start | bytes 9224 | tf_op jit(solution)/shard_map/ppermute | solution.py:29
  18.7 1.3 %fusion.61 = (f32[3,15,16,256]{3,2,1,0:T(8,128)}, f32[3,15,16,256]{3,2,1,0:T(8,128)}) fusion(f32[3,16,16,256]{3,2,1,0:T(8,128)S(1)} %bitcast.51), kind=kLoop, calls=%fused_computation.98 | loop fusion | bytes 2949120 | tf_op jit(solution)/shard_map/slice | solution.py:46
  20.1 1.4 %fusion.64 = (f32[3,16,16,255]{3,2,1,0:T(8,128)}, f32[3,16,16,255]{3,2,1,0:T(8,128)}) fusion(f32[3,16,16,256]{3,2,1,0:T(8,128)S(1)} %bitcast.53), kind=kLoop, calls=%fused_computation.101 | loop fusion | bytes 3133440 | tf_op jit(solution)/shard_map/slice | solution.py:83
  22.9 1.1 add_bitcast_fusion
  24.5 11.8 %collective-permute-done.3 = f32[3,16,16,1]{3,2,1,0:T(8,128)} collective-permute-done((f32[3,16,16,1]{3,2,1,0:T(8,128)}, f32[3,16,16,1]{3,2,1,0:T(8,128)}, u32[]{:S(2)}, u32[]{:S(2)}) %collective-permute-start.3) | collective-permute-done | bytes 3104 | tf_op jit(solution)/shard_map/ppermute | solution.py:29
  36.3 3.2 %fusion = f32[3,16,16,256]{3,2,1,0:T(8,128)S(1)} fusion(f32[3,15,16,256]{3,2,1,0:T(8,128)} %get-tuple-element.50, f32[3,1,16,256]{3,2,1,0:T(8,128)S(1)} %get-tuple-element.5, f32[3,16,1,256]{3,2,1,0:T(1,128)} %collective-permute-done.2, f32[3,16,15,256]{3,2,1,0:T(8,128)S(1)} %get-tuple-element.54, f32[3,16,16,255]{3,2,1,0:T(8,128)} %get-tuple-element.56, ...), kind=kLoop, calls=%fused_computation.5 | loop fusion | flops 4915200 | bytes 8339504 | tf_op jit(solution)/shard_map/add | solution.py:56
  40.5 3.6 %collective-permute-start.6 = (f32[3,16,1,256]{3,2,1,0:T(1,128)S(1)}, f32[3,16,1,256]{3,2,1,0:T(1,128)S(1)}, u32[]{:S(2)}, u32[]{:S(2)}) collective-permute-start(f32[3,16,1,256]{3,2,1,0:T(1,128)S(1)} %get-tuple-element.39), channel_id=1, source_target_pairs={{8,0},{16,8},{24,16},{32,24},{40,32},{48,40},{56,48},{64,56},{72,6... | collective-permute-start | bytes 147464 | tf_op jit(solution)/shard_map/ppermute | solution.py:23
  44.1 2.4 %collective-permute-start.8 = (f32[3,16,16,1]{3,2,1,0:T(8,128)S(1)}, f32[3,16,16,1]{3,2,1,0:T(8,128)S(1)}, u32[]{:S(2)}, u32[]{:S(2)}) collective-permute-start(f32[3,16,16,1]{3,2,1,0:T(8,128)S(1)} %get-tuple-element.44), channel_id=1, source_target_pairs={{1,0},{2,1},{3,2},{4,3},{5,4},{6,5},{7,6},{9,8},{10,9},{11,10},{12... | collective-permute-start | bytes 9224 | tf_op jit(solution)/shard_map/ppermute | solution.py:29
  46.5 1.3 %collective-permute-start.7 = (f32[3,16,16,1]{3,2,1,0:T(8,128)S(1)}, f32[3,16,16,1]{3,2,1,0:T(8,128)S(1)}, u32[]{:S(2)}, u32[]{:S(2)}) collective-permute-start(f32[3,16,16,1]{3,2,1,0:T(8,128)S(1)} %get-tuple-element.45), channel_id=1, source_target_pairs={{0,1},{1,2},{2,3},{3,4},{4,5},{5,6},{6,7},{8,9},{9,10},{10,11},{11... | collective-permute-start | bytes 9224 | tf_op jit(solution)/shard_map/ppermute | solution.py:29
  47.8 5.6 %collective-permute-done.8 = f32[3,16,16,1]{3,2,1,0:T(8,128)S(1)} collective-permute-done((f32[3,16,16,1]{3,2,1,0:T(8,128)S(1)}, f32[3,16,16,1]{3,2,1,0:T(8,128)S(1)}, u32[]{:S(2)}, u32[]{:S(2)}) %collective-permute-start.8) | collective-permute-done | bytes 3104 | tf_op jit(solution)/shard_map/ppermute | solution.py:29
  53.5 11.5 %collective-permute-done.7 = f32[3,16,16,1]{3,2,1,0:T(8,128)S(1)} collective-permute-done((f32[3,16,16,1]{3,2,1,0:T(8,128)S(1)}, f32[3,16,16,1]{3,2,1,0:T(8,128)S(1)}, u32[]{:S(2)}, u32[]{:S(2)}) %collective-permute-start.7) | collective-permute-done | bytes 3104 | tf_op jit(solution)/shard_map/ppermute | solution.py:29
  65.0 1.1 fusion.1
  67.1 3.6 %collective-permute-start.10 = (f32[3,16,1,256]{3,2,1,0:T(1,128)S(1)}, f32[3,16,1,256]{3,2,1,0:T(1,128)S(1)}, u32[]{:S(2)}, u32[]{:S(2)}) collective-permute-start(f32[3,16,1,256]{3,2,1,0:T(1,128)S(1)} %get-tuple-element.26), channel_id=1, source_target_pairs={{8,0},{16,8},{24,16},{32,24},{40,32},{48,40},{56,48},{64,56},{72,6... | collective-permute-start | bytes 147464 | tf_op jit(solution)/shard_map/ppermute | solution.py:23
  70.7 2.4 %collective-permute-start.12 = (f32[3,16,16,1]{3,2,1,0:T(8,128)S(1)}, f32[3,16,16,1]{3,2,1,0:T(8,128)S(1)}, u32[]{:S(2)}, u32[]{:S(2)}) collective-permute-start(f32[3,16,16,1]{3,2,1,0:T(8,128)S(1)} %get-tuple-element.31), channel_id=1, source_target_pairs={{1,0},{2,1},{3,2},{4,3},{5,4},{6,5},{7,6},{9,8},{10,9},{11,10},{12... | collective-permute-start | bytes 9224 | tf_op jit(solution)/shard_map/ppermute | solution.py:29
  73.1 1.5 %collective-permute-start.11 = (f32[3,16,16,1]{3,2,1,0:T(8,128)S(1)}, f32[3,16,16,1]{3,2,1,0:T(8,128)S(1)}, u32[]{:S(2)}, u32[]{:S(2)}) collective-permute-start(f32[3,16,16,1]{3,2,1,0:T(8,128)S(1)} %get-tuple-element.32), channel_id=1, source_target_pairs={{0,1},{1,2},{2,3},{3,4},{4,5},{5,6},{6,7},{8,9},{9,10},{10,11},{11... | collective-permute-start | bytes 9224 | tf_op jit(solution)/shard_map/ppermute | solution.py:29
  74.6 4.0 %collective-permute-done.12 = f32[3,16,16,1]{3,2,1,0:T(8,128)S(1)} collective-permute-done((f32[3,16,16,1]{3,2,1,0:T(8,128)S(1)}, f32[3,16,16,1]{3,2,1,0:T(8,128)S(1)}, u32[]{:S(2)}, u32[]{:S(2)}) %collective-permute-start.12) | collective-permute-done | bytes 3104 | tf_op jit(solution)/shard_map/ppermute | solution.py:29
  78.6 11.5 %collective-permute-done.11 = f32[3,16,16,1]{3,2,1,0:T(8,128)S(1)} collective-permute-done((f32[3,16,16,1]{3,2,1,0:T(8,128)S(1)}, f32[3,16,16,1]{3,2,1,0:T(8,128)S(1)}, u32[]{:S(2)}, u32[]{:S(2)}) %collective-permute-start.11) | collective-permute-done | bytes 3104 | tf_op jit(solution)/shard_map/ppermute | solution.py:29
  90.1 1.1 fusion.2
  92.3 3.6 %collective-permute-start.14 = (f32[3,16,1,256]{3,2,1,0:T(1,128)S(1)}, f32[3,16,1,256]{3,2,1,0:T(1,128)S(1)}, u32[]{:S(2)}, u32[]{:S(2)}) collective-permute-start(f32[3,16,1,256]{3,2,1,0:T(1,128)S(1)} %get-tuple-element.13), channel_id=1, source_target_pairs={{8,0},{16,8},{24,16},{32,24},{40,32},{48,40},{56,48},{64,56},{72,6... | collective-permute-start | bytes 147464 | tf_op jit(solution)/shard_map/ppermute | solution.py:23
  95.8 2.8 %collective-permute-start.16 = (f32[3,16,16,1]{3,2,1,0:T(8,128)S(1)}, f32[3,16,16,1]{3,2,1,0:T(8,128)S(1)}, u32[]{:S(2)}, u32[]{:S(2)}) collective-permute-start(f32[3,16,16,1]{3,2,1,0:T(8,128)S(1)} %get-tuple-element.18), channel_id=1, source_target_pairs={{1,0},{2,1},{3,2},{4,3},{5,4},{6,5},{7,6},{9,8},{10,9},{11,10},{12... | collective-permute-start | bytes 9224 | tf_op jit(solution)/shard_map/ppermute | solution.py:29
  98.6 1.3 %collective-permute-start.15 = (f32[3,16,16,1]{3,2,1,0:T(8,128)S(1)}, f32[3,16,16,1]{3,2,1,0:T(8,128)S(1)}, u32[]{:S(2)}, u32[]{:S(2)}) collective-permute-start(f32[3,16,16,1]{3,2,1,0:T(8,128)S(1)} %get-tuple-element.19), channel_id=1, source_target_pairs={{0,1},{1,2},{2,3},{3,4},{4,5},{5,6},{6,7},{8,9},{9,10},{10,11},{11... | collective-permute-start | bytes 9224 | tf_op jit(solution)/shard_map/ppermute | solution.py:29
  99.9 3.4 %collective-permute-done.16 = f32[3,16,16,1]{3,2,1,0:T(8,128)S(1)} collective-permute-done((f32[3,16,16,1]{3,2,1,0:T(8,128)S(1)}, f32[3,16,16,1]{3,2,1,0:T(8,128)S(1)}, u32[]{:S(2)}, u32[]{:S(2)}) %collective-permute-start.16) | collective-permute-done | bytes 3104 | tf_op jit(solution)/shard_map/ppermute | solution.py:29
  103.3 9.9 %collective-permute-done.15 = f32[3,16,16,1]{3,2,1,0:T(8,128)S(1)} collective-permute-done((f32[3,16,16,1]{3,2,1,0:T(8,128)S(1)}, f32[3,16,16,1]{3,2,1,0:T(8,128)S(1)}, u32[]{:S(2)}, u32[]{:S(2)}) %collective-permute-start.15) | collective-permute-done | bytes 3104 | tf_op jit(solution)/shard_map/ppermute | solution.py:29
  113.1 1.1 fusion.3
  114.3 4.6 %collective-permute-start.17 = (f32[3,16,256]{2,1,0:T(8,128)S(1)}, f32[3,16,256]{2,1,0:T(8,128)S(1)}, u32[]{:S(2)}, u32[]{:S(2)}) collective-permute-start(f32[3,16,256]{2,1,0:T(8,128)S(1)} %slice_bitcast_fusion.12), channel_id=1, source_target_pairs={{0,128},{128,0},{1,129},{129,1},{2,130},{130,2},{3,131},{131,3},{4... | collective-permute-start | bytes 147464 | tf_op jit(solution)/shard_map/ppermute | solution.py:17
  (56 shorter events, 7.4 us)
Async XLA Ops:
  2.5 33.8 %collective-permute-start.1 = (f32[3,16,1,256]{3,2,1,0:T(1,128)}, f32[3,16,1,256]{3,2,1,0:T(1,128)}, u32[]{:S(2)}, u32[]{:S(2)}) collective-permute-start(f32[3,16,1,256]{3,2,1,0:T(1,128)} %get-tuple-element.51), channel_id=1, source_target_pairs={{120,0},{0,8},{8,16},{16,24},{24,32},{32,40},{40,48},{48,56},{56,6... | collective-permute-start | bytes 147464 | tf_op jit(solution)/shard_map/ppermute | solution.py:23
  3.4 32.9 %collective-permute-start.2 = (f32[3,16,1,256]{3,2,1,0:T(1,128)}, f32[3,16,1,256]{3,2,1,0:T(1,128)}, u32[]{:S(2)}, u32[]{:S(2)}) collective-permute-start(f32[3,16,1,256]{3,2,1,0:T(1,128)} %get-tuple-element.52), channel_id=1, source_target_pairs={{8,0},{16,8},{24,16},{32,24},{40,32},{48,40},{56,48},{64,56},{72,6... | collective-permute-start | bytes 147464 | tf_op jit(solution)/shard_map/ppermute | solution.py:23
  10.2 7.6 %copy-start = (f32[1,3,16,16,256]{4,3,2,1,0:T(8,128)S(1)}, f32[1,3,16,16,256]{4,3,2,1,0:T(8,128)}, u32[]{:S(2)}) copy-start(f32[1,3,16,16,256]{4,3,2,1,0:T(8,128)} %param.5) | copy-start | bytes 2359300
  10.2 14.0 %collective-permute-start = (f32[3,2,16,256]{3,2,1,0:T(8,128)}, f32[3,2,16,256]{3,2,1,0:T(8,128)S(1)}, u32[]{:S(2)}, u32[]{:S(2)}) collective-permute-start(f32[3,2,16,256]{3,2,1,0:T(8,128)} %slice.276), channel_id=1, source_target_pairs={{0,128},{128,0},{1,129},{129,1},{2,130},{130,2},{3,131},{131,3},{4... | collective-permute-start | bytes 294920 | tf_op jit(solution)/shard_map/ppermute | solution.py:17
  13.3 11.2 %collective-permute-start.4 = (f32[3,16,16,1]{3,2,1,0:T(8,128)}, f32[3,16,16,1]{3,2,1,0:T(8,128)}, u32[]{:S(2)}, u32[]{:S(2)}) collective-permute-start(f32[3,16,16,1]{3,2,1,0:T(8,128)} %get-tuple-element.57), channel_id=1, source_target_pairs={{1,0},{2,1},{3,2},{4,3},{5,4},{6,5},{7,6},{9,8},{10,9},{11,10},{12... | collective-permute-start | bytes 9224 | tf_op jit(solution)/shard_map/ppermute | solution.py:29
  16.4 19.8 %collective-permute-start.3 = (f32[3,16,16,1]{3,2,1,0:T(8,128)}, f32[3,16,16,1]{3,2,1,0:T(8,128)}, u32[]{:S(2)}, u32[]{:S(2)}) collective-permute-start(f32[3,16,16,1]{3,2,1,0:T(8,128)} %get-tuple-element.58), channel_id=1, source_target_pairs={{0,1},{1,2},{2,3},{3,4},{4,5},{5,6},{6,7},{8,9},{9,10},{10,11},{11... | collective-permute-start | bytes 9224 | tf_op jit(solution)/shard_map/ppermute | solution.py:29
  20.1 2.8 %copy-start.2 = (f32[1,16,16,256]{3,2,1,0:T(8,128)S(1)}, f32[1,16,16,256]{3,2,1,0:T(8,128)}, u32[]{:S(2)}) copy-start(f32[1,16,16,256]{3,2,1,0:T(8,128)} %param.8) | copy-start | bytes 786436
  21.5 0.7 copy-start.5
  22.2 14.0 %copy-start.1 = (f32[1,3,16,16,256]{4,3,2,1,0:T(8,128)S(1)}, f32[1,3,16,16,256]{4,3,2,1,0:T(8,128)}, u32[]{:S(2)}) copy-start(f32[1,3,16,16,256]{4,3,2,1,0:T(8,128)} %param.6) | copy-start | bytes 2359300
  22.9 13.4 %copy-start.3 = (f32[3,16,16,255]{3,2,1,0:T(8,128)S(1)}, f32[3,16,16,255]{3,2,1,0:T(8,128)}, u32[]{:S(2)}) copy-start(f32[3,16,16,255]{3,2,1,0:T(8,128)} %get-tuple-element.55) | copy-start | bytes 2350084
  40.4 24.6 %collective-permute-start.5 = (f32[3,16,1,256]{3,2,1,0:T(1,128)S(1)}, f32[3,16,1,256]{3,2,1,0:T(1,128)S(1)}, u32[]{:S(2)}, u32[]{:S(2)}) collective-permute-start(f32[3,16,1,256]{3,2,1,0:T(1,128)S(1)} %get-tuple-element.38), channel_id=1, source_target_pairs={{120,0},{0,8},{8,16},{16,24},{24,32},{32,40},{40,48},{48,56},{56,6... | collective-permute-start | bytes 147464 | tf_op jit(solution)/shard_map/ppermute | solution.py:23
  40.5 24.5 %collective-permute-start.6 = (f32[3,16,1,256]{3,2,1,0:T(1,128)S(1)}, f32[3,16,1,256]{3,2,1,0:T(1,128)S(1)}, u32[]{:S(2)}, u32[]{:S(2)}) collective-permute-start(f32[3,16,1,256]{3,2,1,0:T(1,128)S(1)} %get-tuple-element.39), channel_id=1, source_target_pairs={{8,0},{16,8},{24,16},{32,24},{40,32},{48,40},{56,48},{64,56},{72,6... | collective-permute-start | bytes 147464 | tf_op jit(solution)/shard_map/ppermute | solution.py:23
  44.1 9.4 %collective-permute-start.8 = (f32[3,16,16,1]{3,2,1,0:T(8,128)S(1)}, f32[3,16,16,1]{3,2,1,0:T(8,128)S(1)}, u32[]{:S(2)}, u32[]{:S(2)}) collective-permute-start(f32[3,16,16,1]{3,2,1,0:T(8,128)S(1)} %get-tuple-element.44), channel_id=1, source_target_pairs={{1,0},{2,1},{3,2},{4,3},{5,4},{6,5},{7,6},{9,8},{10,9},{11,10},{12... | collective-permute-start | bytes 9224 | tf_op jit(solution)/shard_map/ppermute | solution.py:29
  46.5 18.5 %collective-permute-start.7 = (f32[3,16,16,1]{3,2,1,0:T(8,128)S(1)}, f32[3,16,16,1]{3,2,1,0:T(8,128)S(1)}, u32[]{:S(2)}, u32[]{:S(2)}) collective-permute-start(f32[3,16,16,1]{3,2,1,0:T(8,128)S(1)} %get-tuple-element.45), channel_id=1, source_target_pairs={{0,1},{1,2},{2,3},{3,4},{4,5},{5,6},{6,7},{8,9},{9,10},{10,11},{11... | collective-permute-start | bytes 9224 | tf_op jit(solution)/shard_map/ppermute | solution.py:29
  67.0 23.1 %collective-permute-start.9 = (f32[3,16,1,256]{3,2,1,0:T(1,128)S(1)}, f32[3,16,1,256]{3,2,1,0:T(1,128)S(1)}, u32[]{:S(2)}, u32[]{:S(2)}) collective-permute-start(f32[3,16,1,256]{3,2,1,0:T(1,128)S(1)} %get-tuple-element.25), channel_id=1, source_target_pairs={{120,0},{0,8},{8,16},{16,24},{24,32},{32,40},{40,48},{48,56},{56,6... | collective-permute-start | bytes 147464 | tf_op jit(solution)/shard_map/ppermute | solution.py:23
  67.1 23.0 %collective-permute-start.10 = (f32[3,16,1,256]{3,2,1,0:T(1,128)S(1)}, f32[3,16,1,256]{3,2,1,0:T(1,128)S(1)}, u32[]{:S(2)}, u32[]{:S(2)}) collective-permute-start(f32[3,16,1,256]{3,2,1,0:T(1,128)S(1)} %get-tuple-element.26), channel_id=1, source_target_pairs={{8,0},{16,8},{24,16},{32,24},{40,32},{48,40},{56,48},{64,56},{72,6... | collective-permute-start | bytes 147464 | tf_op jit(solution)/shard_map/ppermute | solution.py:23
  70.7 7.9 %collective-permute-start.12 = (f32[3,16,16,1]{3,2,1,0:T(8,128)S(1)}, f32[3,16,16,1]{3,2,1,0:T(8,128)S(1)}, u32[]{:S(2)}, u32[]{:S(2)}) collective-permute-start(f32[3,16,16,1]{3,2,1,0:T(8,128)S(1)} %get-tuple-element.31), channel_id=1, source_target_pairs={{1,0},{2,1},{3,2},{4,3},{5,4},{6,5},{7,6},{9,8},{10,9},{11,10},{12... | collective-permute-start | bytes 9224 | tf_op jit(solution)/shard_map/ppermute | solution.py:29
  73.1 17.0 %collective-permute-start.11 = (f32[3,16,16,1]{3,2,1,0:T(8,128)S(1)}, f32[3,16,16,1]{3,2,1,0:T(8,128)S(1)}, u32[]{:S(2)}, u32[]{:S(2)}) collective-permute-start(f32[3,16,16,1]{3,2,1,0:T(8,128)S(1)} %get-tuple-element.32), channel_id=1, source_target_pairs={{0,1},{1,2},{2,3},{3,4},{4,5},{5,6},{6,7},{8,9},{9,10},{10,11},{11... | collective-permute-start | bytes 9224 | tf_op jit(solution)/shard_map/ppermute | solution.py:29
  92.2 21.0 %collective-permute-start.13 = (f32[3,16,1,256]{3,2,1,0:T(1,128)S(1)}, f32[3,16,1,256]{3,2,1,0:T(1,128)S(1)}, u32[]{:S(2)}, u32[]{:S(2)}) collective-permute-start(f32[3,16,1,256]{3,2,1,0:T(1,128)S(1)} %get-tuple-element.12), channel_id=1, source_target_pairs={{120,0},{0,8},{8,16},{16,24},{24,32},{32,40},{40,48},{48,56},{56,6... | collective-permute-start | bytes 147464 | tf_op jit(solution)/shard_map/ppermute | solution.py:23
  92.3 20.9 %collective-permute-start.14 = (f32[3,16,1,256]{3,2,1,0:T(1,128)S(1)}, f32[3,16,1,256]{3,2,1,0:T(1,128)S(1)}, u32[]{:S(2)}, u32[]{:S(2)}) collective-permute-start(f32[3,16,1,256]{3,2,1,0:T(1,128)S(1)} %get-tuple-element.13), channel_id=1, source_target_pairs={{8,0},{16,8},{24,16},{32,24},{40,32},{48,40},{56,48},{64,56},{72,6... | collective-permute-start | bytes 147464 | tf_op jit(solution)/shard_map/ppermute | solution.py:23
  95.8 7.4 %collective-permute-start.16 = (f32[3,16,16,1]{3,2,1,0:T(8,128)S(1)}, f32[3,16,16,1]{3,2,1,0:T(8,128)S(1)}, u32[]{:S(2)}, u32[]{:S(2)}) collective-permute-start(f32[3,16,16,1]{3,2,1,0:T(8,128)S(1)} %get-tuple-element.18), channel_id=1, source_target_pairs={{1,0},{2,1},{3,2},{4,3},{5,4},{6,5},{7,6},{9,8},{10,9},{11,10},{12... | collective-permute-start | bytes 9224 | tf_op jit(solution)/shard_map/ppermute | solution.py:29
  98.6 14.5 %collective-permute-start.15 = (f32[3,16,16,1]{3,2,1,0:T(8,128)S(1)}, f32[3,16,16,1]{3,2,1,0:T(8,128)S(1)}, u32[]{:S(2)}, u32[]{:S(2)}) collective-permute-start(f32[3,16,16,1]{3,2,1,0:T(8,128)S(1)} %get-tuple-element.19), channel_id=1, source_target_pairs={{0,1},{1,2},{2,3},{3,4},{4,5},{5,6},{6,7},{8,9},{9,10},{10,11},{11... | collective-permute-start | bytes 9224 | tf_op jit(solution)/shard_map/ppermute | solution.py:29
  114.3 6.1 %copy-start.4 = (f32[3,16,16,256]{3,2,1,0:T(8,128)}, f32[3,16,16,256]{3,2,1,0:T(8,128)S(1)}, u32[]{:S(2)}) copy-start(f32[3,16,16,256]{3,2,1,0:T(8,128)S(1)} %fusion.3) | copy-start | bytes 2359300
  114.3 5.5 %collective-permute-start.17 = (f32[3,16,256]{2,1,0:T(8,128)S(1)}, f32[3,16,256]{2,1,0:T(8,128)S(1)}, u32[]{:S(2)}, u32[]{:S(2)}) collective-permute-start(f32[3,16,256]{2,1,0:T(8,128)S(1)} %slice_bitcast_fusion.12), channel_id=1, source_target_pairs={{0,128},{128,0},{1,129},{129,1},{2,130},{130,2},{3,131},{131,3},{4... | collective-permute-start | bytes 147464 | tf_op jit(solution)/shard_map/ppermute | solution.py:17
where the time goes:
time: 121 us; the launch traced here: 120 us
  waiting for transfers between devices  58.8 us (49%)
  starting transfers between devices  38.8 us (32%)
  local copies, waits for them, and re-layouts  13.5 us (11%)
  other arithmetic  8.32 us (7%)
    ppermute x8, waiting for transfers between devices, passed_along(): lax.ppermute(value, axis, [(source, source + steps) for source in range(f...  57.9 us
    ppermute x8, starting transfers between devices, shifted(): return lax.ppermute(block, axis, route)  17.1 us
    ppermute x8, starting transfers between devices, passed_along(): lax.ppermute(value, axis, [(source, source + steps) for source in range(f...  16.1 us
    add x4, other arithmetic, relax(): return center + OMEGA * residual / scale  6.55 us
    ppermute x2, starting transfers between devices, from_partner(): return lax.ppermute(value, axis, pairs)  5.55 us
    slice x4, local copies, waits for them, and re-layouts, local(): from_north = passed_along(current[..., :1], 'gy', -1)  2.61 us
  transfers between devices with their start and end apart: 18, of which 9 were waited for; matrix products, arithmetic and copies ran while one was open for 8% of the time, Pallas kernels for 0%

commit v1 on v0

v1 whole, which is shorter than its diff:
```python
import functools

import jax
import jax.numpy as jnp
from jax import lax
from jax.experimental import pallas as pl
from jax.experimental.pallas import tpu as pltpu
from jax.sharding import PartitionSpec as P

SWEEPS = 4
K = 3
OMEGA = 0.8
RATIO = 0.5
THETA = 0.7
LANES = 128
MESH = pl.DeviceIdType.MESH


def kernel(
    nx,
    ny,
    L,
    X,
    GROUPS,
    f_ref,
    s_ref,
    r_ref,
    v_ref,
    c_ref,
    o_ref,
    i_ref,
    F,
    S,
    RV,
    U,
    W,
    V1,
    SS,
    YO,
    YI,
    M,
    GH,
    O,
    PR,
    IO,
    f_sem,
    s_sem,
    rv_sem,
    o_sem,
    i_sem,
    xs_sem,
    xr_sem,
    ys_sem,
    yr_sem,
    p_sem,
    C,
    c_sem,
):
    side = lax.axis_index("side")
    gx = lax.axis_index("gx")
    gy = lax.axis_index("gy")
    fluid = side == 0
    west = (side, lax.rem(gx + nx - 1, nx), gy)
    east = (side, lax.rem(gx + 1, nx), gy)
    south = (side, gx, gy - 1)
    north = (side, gx, gy + 1)
    partner = (1 - side, gx, gy)
    has_south = gy > 0
    has_north = gy < ny - 1
    pairs = X // 2 // GROUPS

    barrier = pltpu.get_barrier_semaphore()

    def greet(device):
        pl.semaphore_signal(barrier, inc=1, device_id=device, device_id_type=MESH)

    greet(west)
    greet(east)
    greet(partner)
    pl.when(has_south)(lambda: greet(south))
    pl.when(has_north)(lambda: greet(north))

    def half(ref, h):
        return ref.at[..., pl.ds(h * LANES, LANES)]

    loads_f = [pltpu.make_async_copy(half(f_ref, h), F.at[h], f_sem.at[h]) for h in range(2)]
    loads_s = [pltpu.make_async_copy(half(s_ref, h), S.at[h], s_sem.at[h]) for h in range(2)]
    loads_rv = [
        pltpu.make_async_copy(half(ref, h), RV.at[n, h], rv_sem.at[n, h])
        for n, ref in enumerate((r_ref, v_ref))
        for h in range(2)
    ]
    load_c = pltpu.make_async_copy(c_ref, C, c_sem)
    for copy in loads_f + loads_rv + loads_s + [load_c]:
        copy.start()

    lane = lax.broadcasted_iota(jnp.int32, (8, LANES), 1)
    wide_lane = lax.broadcasted_iota(jnp.int32, (L, LANES), 1)
    row = lax.broadcasted_iota(jnp.int32, (L, LANES), 0)
    zero = jnp.zeros((8, LANES), jnp.float32)

    def x_copy(t, d):
        source, target = ((X, 0), (1, X + 1))[d]
        return pltpu.make_async_remote_copy(
            U.at[t, :, :, source],
            U.at[t, :, :, target],
            xs_sem.at[t, d],
            xr_sem.at[t, d],
            device_id=(east, west)[d],
            device_id_type=MESH,
        )

    def y_copy(t, g, d):
        return pltpu.make_async_remote_copy(
            YO.at[t, g, d],
            YI.at[t, g, d],
            ys_sem.at[t, g, d],
            yr_sem.at[t, g, d],
            device_id=(north, south)[d],
            device_id_type=MESH,
        )

    def y_start(t, g):
        pl.when(has_north)(lambda: y_copy(t, g, 0).start())
        pl.when(has_south)(lambda: y_copy(t, g, 1).start())

    def y_wait(t, g):
        pl.when(has_south)(lambda: y_copy(t, g, 0).wait_recv())
        pl.when(has_north)(lambda: y_copy(t, g, 1).wait_recv())

    def packed(columns, first, last, slot):
        to_north, to_south = columns
        for part in range(2):
            place = slot * 2 + part
            rows = slice(8 * part, 8 * part + 8)
            to_north = jnp.where(lane == place, pltpu.roll(last[rows], place + 1, 1), to_north)
            moved = pltpu.roll(first[rows], place, 1) if place else first[rows]
            to_south = jnp.where(lane == place, moved, to_south)
        return to_north, to_south

    def unpacked(packet, slot, target):
        parts = []
        for part in range(2):
            shift = (target - (slot * 2 + part)) % LANES
            parts.append(pltpu.roll(packet, shift, 1) if shift else packet)
        return jnp.concatenate(parts, axis=0)

    def rows_of(g):
        for n in range(pairs):
            pair = g * pairs + n
            yield pair, 2 * n
            yield X - 1 - pair, 2 * n + 1

    for copy in loads_f:
        copy.wait()

    for h in range(2):
        for k in range(K):
            layer0, layer1 = F[h, k, 0:X], F[h, k, X : 2 * X]
            M[h, k] = jnp.where(fluid, RATIO * (layer1 - layer0), layer0)

    def stage(g, carry):
        columns = (zero, zero)
        for x, number in rows_of(g):
            for k in range(K):
                tiles = []
                for h in range(2):
                    tile = jnp.concatenate(
                        [
                            F[h, k, pl.ds(8 * part * X + x, 8, stride=X), :]
                            for part in range(2)
                        ],
                        axis=0,
                    )
                    U[0, h, k, x + 1] = tile
                    tiles.append(tile)
                columns = packed(columns, tiles[0], tiles[1], number * K + k)
        YO[0, g, 0], YO[0, g, 1] = columns
        return carry

    lax.fori_loop(0, GROUPS, stage, 0)

    greeted = 3 + has_south.astype(jnp.int32) + has_north.astype(jnp.int32)
    pl.semaphore_wait(barrier, greeted)

    for g in range(GROUPS):
        y_start(0, g)
    for d in range(2):
        x_copy(0, d).start()
    ghosts = pltpu.make_async_remote_copy(
        M, GH, p_sem.at[0], p_sem.at[1], device_id=partner, device_id_type=MESH
    )
    ghosts.start()

    def blank(d):
        for t in range(SWEEPS):
            for g in range(GROUPS):
                YI[t, g, d] = zero

    pl.when(jnp.logical_not(has_south))(lambda: blank(0))
    pl.when(jnp.logical_not(has_north))(lambda: blank(1))

    for copy in loads_rv + loads_s + [load_c]:
        copy.wait()
    mix = [[C[k, 0, j] for j in range(K)] for k in range(K)]

    def weigh(x, carry):
        for h in range(2):
            for part in range(2):
                rows = pl.ds(8 * part * X + x, 8, stride=X)
                out = pl.ds(8 * part, 8)
                speed = RV[1, h, rows, :]
                diag = 6.0 + RV[0, h, rows, :] + speed
                V1[h, x, out] = 1.0 + speed
                for k in range(K):
                    W[h, k, x, out] = OMEGA / (diag + mix[k][k])
                    SS[h, k, x, out] = S[h, k, rows, :]
        return carry

    lax.fori_loop(0, X, weigh, 0)

    ghosts.wait()
    own = jnp.where(fluid, 0.0, 1.0)

    def relax(t, g, x, number):
        speeds = [V1[h, x] for h in range(2)]
        center = [[U[t, h, k, x + 1] for h in range(2)] for k in range(K)]
        new = []
        for k in range(K):
            slot = number * K + k
            from_south = unpacked(YI[t, g, 0], slot, 0)
            from_north = unpacked(YI[t, g, 1], slot, LANES - 1)
            up = [pltpu.roll(center[k][h], 1, 1) for h in range(2)]
            down = [pltpu.roll(center[k][h], LANES - 1, 1) for h in range(2)]
            souths = (
                jnp.where(wide_lane == 0, from_south, up[0]),
                jnp.where(wide_lane == 0, up[0], up[1]),
            )
            norths = (
                jnp.where(wide_lane == LANES - 1, down[1], down[0]),
                jnp.where(wide_lane == LANES - 1, from_north, down[1]),
            )
            results = []
            for h in range(2):
                here = center[k][h]
                ghost = own * here + GH[h, k, pl.ds(x, 1), :]
                below = jnp.where(row == 0, ghost, pltpu.roll(here, 1, 0))
                above = jnp.where(row == L - 1, 0.0, pltpu.roll(here, L - 1, 0))
                total = SS[h, k, x] + below + above
                total = total + speeds[h] * U[t, h, k, x] + U[t, h, k, x + 2]
                total = total + souths[h] + norths[h]
                for j in range(K):
                    if j != k:
                        total = total - mix[k][j] * center[j][h]
                results.append((1.0 - OMEGA) * here + W[h, k, x] * total)
            new.append(results)
        return new

    def sweep(t, carry):
        for d in range(2):
            x_copy(t, d).wait_recv()

        def group(g, carry):
            y_wait(t, g)
            columns = (zero, zero)
            for x, number in rows_of(g):
                new = relax(t, g, x, number)
                for k in range(K):
                    for h in range(2):
                        U[t + 1, h, k, x + 1] = new[k][h]
                    columns = packed(columns, new[k][0], new[k][1], number * K + k)
                if number == 1:

                    @pl.when(g == 0)
                    def _():
                        for d in range(2):
                            x_copy(t + 1, d).start()

            YO[t + 1, g, 0], YO[t + 1, g, 1] = columns
            y_start(t + 1, g)
            return carry

        lax.fori_loop(0, GROUPS, group, 0)
        return carry

    lax.fori_loop(0, SWEEPS - 1, sweep, 0)

    last = SWEEPS - 1
    for d in range(2):
        x_copy(last, d).wait_recv()

    def finish(g, carry):
        y_wait(last, g)
        for x, number in rows_of(g):
            new = relax(last, g, x, number)
            for k in range(K):
                for h in range(2):
                    for part in range(2):
                        rows = pl.ds(8 * part * X + x, 8, stride=X)
                        O[h, k, rows, :] = new[k][h][8 * part : 8 * part + 8]
        return carry

    lax.fori_loop(0, GROUPS, finish, 0)

    traces = pltpu.make_async_remote_copy(
        O.at[:, :, pl.ds(0, X)], PR, p_sem.at[2], p_sem.at[3], device_id=partner, device_id_type=MESH
    )
    traces.start()
    stores = [pltpu.make_async_copy(O.at[h], half(o_ref, h), o_sem.at[h]) for h in range(2)]
    for copy in stores:
        copy.start()

    for t in range(SWEEPS):
        for d in range(2):
            x_copy(t, d).wait_send()

    def sent(n, carry):
        t, g = n // GROUPS, lax.rem(n, GROUPS)
        pl.when(has_north)(lambda: y_copy(t, g, 0).wait_send())
        pl.when(has_south)(lambda: y_copy(t, g, 1).wait_send())
        return carry

    lax.fori_loop(0, SWEEPS * GROUPS, sent, 0)

    traces.wait()
    mine = jnp.where(fluid, 1.0 - THETA, THETA)
    other = jnp.where(fluid, THETA, 1.0 - THETA)
    for h in range(2):
        for k in range(K):
            IO[h, k] = mine * O[h, k, 0:X] + other * PR[h, k]
    edges = [pltpu.make_async_copy(IO.at[h], half(i_ref, h), i_sem.at[h]) for h in range(2)]
    for copy in edges:
        copy.start()
    for copy in stores + edges:
        copy.wait()


def solution(mesh):
    nx, ny = mesh.shape["gx"], mesh.shape["gy"]

    def local(fields, source, reaction, velocity, coupling):
        _, _, L, X, Y = fields.shape
        groups = 4
        f32 = jnp.float32
        cells = L * X
        new, interface = pl.pallas_call(
            functools.partial(kernel, nx, ny, L, X, groups),
            out_shape=(
                jax.ShapeDtypeStruct((K, cells, Y), f32),
                jax.ShapeDtypeStruct((K, X, Y), f32),
            ),
            in_specs=[pl.BlockSpec(memory_space=pltpu.HBM)] * 5,
            out_specs=[pl.BlockSpec(memory_space=pl.ANY)] * 2,
            scratch_shapes=[
                pltpu.VMEM((2, K, cells, LANES), f32),
                pltpu.VMEM((2, K, cells, LANES), f32),
                pltpu.VMEM((2, 2, cells, LANES), f32),
                pltpu.VMEM((SWEEPS, 2, K, X + 2, L, LANES), f32),
                pltpu.VMEM((2, K, X, L, LANES), f32),
                pltpu.VMEM((2, X, L, LANES), f32),
                pltpu.VMEM((2, K, X, L, LANES), f32),
                pltpu.VMEM((SWEEPS, groups, 2, 8, LANES), f32),
                pltpu.VMEM((SWEEPS, groups, 2, 8, LANES), f32),
                pltpu.VMEM((2, K, X, LANES), f32),
                pltpu.VMEM((2, K, X, LANES), f32),
                pltpu.VMEM((2, K, cells, LANES), f32),
                pltpu.VMEM((2, K, X, LANES), f32),
                pltpu.VMEM((2, K, X, LANES), f32),
                pltpu.SemaphoreType.DMA((2,)),
                pltpu.SemaphoreType.DMA((2,)),
                pltpu.SemaphoreType.DMA((2, 2)),
                pltpu.SemaphoreType.DMA((2,)),
                pltpu.SemaphoreType.DMA((2,)),
                pltpu.SemaphoreType.DMA((SWEEPS, 2)),
                pltpu.SemaphoreType.DMA((SWEEPS, 2)),
                pltpu.SemaphoreType.DMA((SWEEPS, groups, 2)),
                pltpu.SemaphoreType.DMA((SWEEPS, groups, 2)),
                pltpu.SemaphoreType.DMA((4,)),
                pltpu.SMEM((K, 1, K), f32),
                pltpu.SemaphoreType.DMA,
            ],
            compiler_params=pltpu.CompilerParams(
                collective_id=0,
                has_side_effects=True,
                vmem_limit_bytes=60 * 1024 * 1024,
            ),
        )(
            fields.reshape(K, cells, Y),
            source.reshape(K, cells, Y),
            reaction.reshape(cells, Y),
            velocity.reshape(cells, Y),
            coupling.reshape(K, 1, K),
        )
        return new.reshape(1, K, L, X, Y), interface[None]

    return jax.shard_map(
        local,
        mesh=mesh,
        in_specs=(
            P("side", None, None, "gx", "gy"),
            P("side", None, None, "gx", "gy"),
            P("side", None, "gx", "gy"),
            P("side", None, "gx", "gy"),
            P("side", None, None),
        ),
        out_specs=(P("side", None, None, "gx", "gy"), P("side", None, "gx", "gy")),
        check_vma=False,
    )
```

time: 121 us -> 36 us (0.30)
  the two profiles are of different devices: /device:TPU:29 before, /device:TPU:1 now
where the time goes in v1:
time: 36 us; the launch traced here: 35.8 us
  Pallas kernels  32.5 us (90%)
  local copies, waits for them, and re-layouts  2.7 us (8%)
  between operations  0.65 us (2%)
    pallas_call x1, Pallas kernels, local(): pl.pallas_call(functools.partial(kernel, nx, ny, L, X, groups), out_shape...  32.5 us
    unnamed x4, local copies, waits for them, and re-layouts  2.7 us

profile of v1, /device:TPU:1, one launch (start us, length us, event | category | flops | bytes accessed | tf_op | source)
XLA Modules:
  0.0 35.8 jit_solution(9289094098623987966)
XLA Ops:
  0.6 32.5 %shard_map.68 = (f32[3,256,256]{2,1,0:T(8,128)}, f32[3,16,256]{2,1,0:T(8,128)}) custom-call(f32[3,256,256]{2,1,0:T(8,128)} %bitcast.7, f32[3,256,256]{2,1,0:T(8,128)} %bitcast.8, f32[256,256]{1,0:T(8,128)} %bitcast.10, f32[256,256]{1,0:T(8,128)} %bitcast.11, f32[3,1,3]{2,1,0:T(1,128)} %bitcast.13), custom_call_target="tpu_custom_call" | custom-call | tf_op jit(solution)/shard_map/pallas_call | solution.py:346
  33.1 0.0 copy-start
  33.1 2.1 %copy.9 = f32[1,3,16,16,256]{4,3,2,1,0:T(8,128)} copy(f32[1,3,16,16,256]{4,3,2,1,0:T(8,128)} %bitcast.9) | data formatting | bytes 1572864
  35.2 0.0 copy-done
  35.2 0.6 %copy.10 = f32[1,3,16,256]{3,2,1,0:T(8,128)} copy(f32[1,3,16,256]{3,2,1,0:T(8,128)S(1)} %bitcast.12) | data formatting | bytes 98304
Async XLA Ops:
  33.1 2.1 %copy-start = (f32[3,16,256]{2,1,0:T(8,128)S(1)}, f32[3,16,256]{2,1,0:T(8,128)}, u32[]{:S(2)}) copy-start(f32[3,16,256]{2,1,0:T(8,128)} %get-tuple-element.5) | copy-start | bytes 147460

commit v2 on v1

--- a/solution.py
+++ b/solution.py
@@ -21,14 +21,14 @@
     ny,
     L,
     X,
-    GROUPS,
+    SPANS,
     f_ref,
     s_ref,
     r_ref,
     v_ref,
     c_ref,
-    o_ref,
-    i_ref,
+    O,
+    IO,
     F,
     S,
     RV,
@@ -40,14 +40,10 @@
     YI,
     M,
     GH,
-    O,
     PR,
-    IO,
     f_sem,
     s_sem,
     rv_sem,
-    o_sem,
-    i_sem,
     xs_sem,
     xr_sem,
     ys_sem,
@@ -67,7 +63,7 @@
     partner = (1 - side, gx, gy)
     has_south = gy > 0
     has_north = gy < ny - 1
-    pairs = X // 2 // GROUPS
+    groups = len(SPANS)
 
     barrier = pltpu.get_barrier_semaphore()
 
@@ -120,6 +116,10 @@
             device_id_type=MESH,
         )
 
+    def x_both(t, step):
+        for d in range(2):
+            getattr(x_copy(t, d), step)()
+
     def y_start(t, g):
         pl.when(has_north)(lambda: y_copy(t, g, 0).start())
         pl.when(has_south)(lambda: y_copy(t, g, 1).start())
@@ -127,6 +127,12 @@
     def y_wait(t, g):
         pl.when(has_south)(lambda: y_copy(t, g, 0).wait_recv())
         pl.when(has_north)(lambda: y_copy(t, g, 1).wait_recv())
+
+    def sent(t):
+        x_both(t, "wait_send")
+        for g in range(groups):
+            pl.when(has_north)(lambda: y_copy(t, g, 0).wait_send())
+            pl.when(has_south)(lambda: y_copy(t, g, 1).wait_send())
 
     def packed(columns, first, last, slot):
         to_north, to_south = columns
@@ -146,10 +152,10 @@
         return jnp.concatenate(parts, axis=0)
 
     def rows_of(g):
-        for n in range(pairs):
-            pair = g * pairs + n
-            yield pair, 2 * n
-            yield X - 1 - pair, 2 * n + 1
+        start = sum(SPANS[:g])
+        for n in range(SPANS[g]):
+            yield start + n, 2 * n
+            yield X - 1 - start - n, 2 * n + 1
 
     for copy in loads_f:
         copy.wait()
@@ -159,7 +165,7 @@
             layer0, layer1 = F[h, k, 0:X], F[h, k, X : 2 * X]
             M[h, k] = jnp.where(fluid, RATIO * (layer1 - layer0), layer0)
 
-    def stage(g, carry):
+    for g in range(groups):
         columns = (zero, zero)
         for x, number in rows_of(g):
             for k in range(K):
@@ -176,17 +182,13 @@
                     tiles.append(tile)
                 columns = packed(columns, tiles[0], tiles[1], number * K + k)
         YO[0, g, 0], YO[0, g, 1] = columns
-        return carry
-
-    lax.fori_loop(0, GROUPS, stage, 0)
 
     greeted = 3 + has_south.astype(jnp.int32) + has_north.astype(jnp.int32)
     pl.semaphore_wait(barrier, greeted)
 
-    for g in range(GROUPS):
+    for g in range(groups):
         y_start(0, g)
-    for d in range(2):
-        x_copy(0, d).start()
+    x_both(0, "start")
     ghosts = pltpu.make_async_remote_copy(
         M, GH, p_sem.at[0], p_sem.at[1], device_id=partner, device_id_type=MESH
     )
@@ -194,7 +196,7 @@
 
     def blank(d):
         for t in range(SWEEPS):
-            for g in range(GROUPS):
+            for g in range(groups):
                 YI[t, g, d] = zero
 
     pl.when(jnp.logical_not(has_south))(lambda: blank(0))
@@ -257,11 +259,10 @@
         return new
 
     def sweep(t, carry):
-        for d in range(2):
-            x_copy(t, d).wait_recv()
-
-        def group(g, carry):
+        for g in range(groups):
             y_wait(t, g)
+            if g == 0:
+                x_both(t, "wait_recv")
             columns = (zero, zero)
             for x, number in rows_of(g):
                 new = relax(t, g, x, number)
@@ -269,28 +270,20 @@
                     for h in range(2):
                         U[t + 1, h, k, x + 1] = new[k][h]
                     columns = packed(columns, new[k][0], new[k][1], number * K + k)
-                if number == 1:
-
-                    @pl.when(g == 0)
-                    def _():
-                        for d in range(2):
-                            x_copy(t + 1, d).start()
-
+                if g == 0 and number == 1:
+                    x_both(t + 1, "start")
             YO[t + 1, g, 0], YO[t + 1, g, 1] = columns
             y_start(t + 1, g)
-            return carry
-
-        lax.fori_loop(0, GROUPS, group, 0)
+        sent(t)
         return carry
 
     lax.fori_loop(0, SWEEPS - 1, sweep, 0)
 
     last = SWEEPS - 1
-    for d in range(2):
-        x_copy(last, d).wait_recv()
-
-    def finish(g, carry):
+    for g in range(groups):
         y_wait(last, g)
+        if g == 0:
+            x_both(last, "wait_recv")
         for x, number in rows_of(g):
             new = relax(last, g, x, number)
             for k in range(K):
@@ -298,40 +291,31 @@
                     for part in range(2):
                         rows = pl.ds(8 * part * X + x, 8, stride=X)
                         O[h, k, rows, :] = new[k][h][8 * part : 8 * part + 8]
-        return carry
-
-    lax.fori_loop(0, GROUPS, finish, 0)
 
     traces = pltpu.make_async_remote_copy(
         O.at[:, :, pl.ds(0, X)], PR, p_sem.at[2], p_sem.at[3], device_id=partner, device_id_type=MESH
     )
     traces.start()
-    stores = [pltpu.make_async_copy(O.at[h], half(o_ref, h), o_sem.at[h]) for h in range(2)]
-    for copy in stores:
-        copy.start()
-
-    for t in range(SWEEPS):
-        for d in range(2):
-            x_copy(t, d).wait_send()
-
-    def sent(n, carry):
-        t, g = n // GROUPS, lax.rem(n, GROUPS)
-        pl.when(has_north)(lambda: y_copy(t, g, 0).wait_send())
-        pl.when(has_south)(lambda: y_copy(t, g, 1).wait_send())
-        return carry
-
-    lax.fori_loop(0, SWEEPS * GROUPS, sent, 0)
-
+    sent(last)
     traces.wait()
     mine = jnp.where(fluid, 1.0 - THETA, THETA)
     other = jnp.where(fluid, THETA, 1.0 - THETA)
     for h in range(2):
         for k in range(K):
             IO[h, k] = mine * O[h, k, 0:X] + other * PR[h, k]
-    edges = [pltpu.make_async_copy(IO.at[h], half(i_ref, h), i_sem.at[h]) for h in range(2)]
-    for copy in edges:
+
+
+def write(a_ref, b_ref, o_ref, i_ref, sem):
+    copies = [
+        pltpu.make_async_copy(
+            tile_ref.at[h], out_ref.at[..., pl.ds(h * LANES, LANES)], sem.at[n, h]
+        )
+        for n, (tile_ref, out_ref) in enumerate(((a_ref, o_ref), (b_ref, i_ref)))
+        for h in range(2)
+    ]
+    for copy in copies:
         copy.start()
-    for copy in stores + edges:
+    for copy in copies:
         copy.wait()
 
 
@@ -340,17 +324,18 @@
 
     def local(fields, source, reaction, velocity, coupling):
         _, _, L, X, Y = fields.shape
-        groups = 4
+        spans = (2, 6)
+        groups = len(spans)
         f32 = jnp.float32
         cells = L * X
-        new, interface = pl.pallas_call(
-            functools.partial(kernel, nx, ny, L, X, groups),
+        tiles, edges = pl.pallas_call(
+            functools.partial(kernel, nx, ny, L, X, spans),
             out_shape=(
-                jax.ShapeDtypeStruct((K, cells, Y), f32),
-                jax.ShapeDtypeStruct((K, X, Y), f32),
+                pltpu.VMEM((2, K, cells, LANES), f32),
+                pltpu.VMEM((2, K, X, LANES), f32),
             ),
             in_specs=[pl.BlockSpec(memory_space=pltpu.HBM)] * 5,
-            out_specs=[pl.BlockSpec(memory_space=pl.ANY)] * 2,
+            out_specs=[pl.BlockSpec(memory_space=pltpu.VMEM)] * 2,
             scratch_shapes=[
                 pltpu.VMEM((2, K, cells, LANES), f32),
                 pltpu.VMEM((2, K, cells, LANES), f32),
@@ -363,14 +348,10 @@
                 pltpu.VMEM((SWEEPS, groups, 2, 8, LANES), f32),
                 pltpu.VMEM((2, K, X, LANES), f32),
                 pltpu.VMEM((2, K, X, LANES), f32),
-                pltpu.VMEM((2, K, cells, LANES), f32),
-                pltpu.VMEM((2, K, X, LANES), f32),
                 pltpu.VMEM((2, K, X, LANES), f32),
                 pltpu.SemaphoreType.DMA((2,)),
                 pltpu.SemaphoreType.DMA((2,)),
                 pltpu.SemaphoreType.DMA((2, 2)),
-                pltpu.SemaphoreType.DMA((2,)),
-                pltpu.SemaphoreType.DMA((2,)),
                 pltpu.SemaphoreType.DMA((SWEEPS, 2)),
                 pltpu.SemaphoreType.DMA((SWEEPS, 2)),
                 pltpu.SemaphoreType.DMA((SWEEPS, groups, 2)),
@@ -391,6 +372,19 @@
             velocity.reshape(cells, Y),
             coupling.reshape(K, 1, K),
         )
+        tiles, edges = (
+            pltpu.with_memory_space_constraint(value, pltpu.VMEM) for value in (tiles, edges)
+        )
+        new, interface = pl.pallas_call(
+            write,
+            out_shape=(
+                jax.ShapeDtypeStruct((K, cells, Y), f32),
+                jax.ShapeDtypeStruct((K, X, Y), f32),
+            ),
+            in_specs=[pl.BlockSpec(memory_space=pltpu.VMEM)] * 2,
+            out_specs=[pl.BlockSpec(memory_space=pltpu.HBM)] * 2,
+            scratch_shapes=[pltpu.SemaphoreType.DMA((2, 2))],
+        )(tiles, edges)
         return new.reshape(1, K, L, X, Y), interface[None]
 
     return jax.shard_map(

time: 36 us -> 33.1 us (0.919)
  local copies, waits for them, and re-layouts: 2.7 us -> 0 us
    unnamed x4 -> x0, local copies, waits for them, and re-layouts: 2.7 us -> none
    pallas_call x1 -> x2, Pallas kernels: 32.5 us -> 32.4 us  [the longest x1 31.5 us: local(): pl.pallas_call(functools.partial(kernel, nx, ny, L, X, spans), out_shape=...]
where the time goes in v2:
time: 33.1 us; the launch traced here: 33 us
  Pallas kernels  32.4 us (98%)
  between operations  0.64 us (2%)
    pallas_call x1, Pallas kernels, local(): pl.pallas_call(functools.partial(kernel, nx, ny, L, X, spans), out_shape=...  31.5 us
    pallas_call x1, Pallas kernels, local(): pl.pallas_call(write, out_shape=(jax.ShapeDtypeStruct((K, cells, Y), f32)...  0.92 us

profile of v2, /device:TPU:1, one launch (start us, length us, event | category | flops | bytes accessed | tf_op | source)
XLA Modules:
  0.0 33.0 jit_solution(17643596476749996738)
XLA Ops:
  0.6 31.5 %shard_map.68 = (f32[2,3,256,128]{3,2,1,0:T(8,128)S(1)}, f32[2,3,16,128]{3,2,1,0:T(8,128)S(1)}) custom-call(f32[3,256,256]{2,1,0:T(8,128)} %bitcast.7, f32[3,256,256]{2,1,0:T(8,128)} %bitcast.8, f32[256,256]{1,0:T(8,128)} %bitcast.9, f32[256,256]{1,0:T(8,128)} %bitcast.10, f32[3,1,3]{2,1,0:T(1,128)} %bitcast.11), custom_call_target="tpu_custom_call" | custom-call | tf_op jit(solution)/shard_map/pallas_call | solution.py:331
  32.1 0.9 %shard_map.69 = (f32[3,256,256]{2,1,0:T(8,128)}, f32[3,16,256]{2,1,0:T(8,128)}) custom-call(f32[2,3,256,128]{3,2,1,0:T(8,128)S(1)} %get-tuple-element.6.a_ref, f32[2,3,16,128]{3,2,1,0:T(8,128)S(1)} %get-tuple-element.7.b_ref), custom_call_target="tpu_custom_call" | custom-call | tf_op jit(solution)/shard_map/pallas_call | solution.py:378

commit v3 on v2

--- a/solution.py
+++ b/solution.py
@@ -98,8 +98,8 @@
     def x_copy(t, d):
         source, target = ((X, 0), (1, X + 1))[d]
         return pltpu.make_async_remote_copy(
-            U.at[t, :, :, source],
-            U.at[t, :, :, target],
+            U.at[t, source],
+            U.at[t, target],
             xs_sem.at[t, d],
             xr_sem.at[t, d],
             device_id=(east, west)[d],
@@ -147,8 +147,8 @@
     def unpacked(packet, slot, target):
         parts = []
         for part in range(2):
-            shift = (target - (slot * 2 + part)) % LANES
-            parts.append(pltpu.roll(packet, shift, 1) if shift else packet)
+            shift = lax.rem(target + LANES - (slot * 2 + part), LANES)
+            parts.append(pltpu.roll(packet, shift, 1))
         return jnp.concatenate(parts, axis=0)
 
     def rows_of(g):
@@ -178,7 +178,7 @@
                         ],
                         axis=0,
                     )
-                    U[0, h, k, x + 1] = tile
+                    U[0, x + 1, h, k] = tile
                     tiles.append(tile)
                 columns = packed(columns, tiles[0], tiles[1], number * K + k)
         YO[0, g, 0], YO[0, g, 1] = columns
@@ -226,7 +226,7 @@
 
     def relax(t, g, x, number):
         speeds = [V1[h, x] for h in range(2)]
-        center = [[U[t, h, k, x + 1] for h in range(2)] for k in range(K)]
+        center = [[U[t, x + 1, h, k] for h in range(2)] for k in range(K)]
         new = []
         for k in range(K):
             slot = number * K + k
@@ -249,7 +249,7 @@
                 below = jnp.where(row == 0, ghost, pltpu.roll(here, 1, 0))
                 above = jnp.where(row == L - 1, 0.0, pltpu.roll(here, L - 1, 0))
                 total = SS[h, k, x] + below + above
-                total = total + speeds[h] * U[t, h, k, x] + U[t, h, k, x + 2]
+                total = total + speeds[h] * U[t, x, h, k] + U[t, x + 2, h, k]
                 total = total + souths[h] + norths[h]
                 for j in range(K):
                     if j != k:
@@ -258,21 +258,39 @@
             new.append(results)
         return new
 
+    def advance(t, g, x, number):
+        new = relax(t, g, x, number)
+        for k in range(K):
+            for h in range(2):
+                U[t + 1, x + 1, h, k] = new[k][h]
+
+    def gather(t, g):
+        columns = (zero, zero)
+        for x, number in rows_of(g):
+            for k in range(K):
+                columns = packed(columns, U[t, x + 1, 0, k], U[t, x + 1, 1, k], number * K + k)
+        YO[t, g, 0], YO[t, g, 1] = columns
+
     def sweep(t, carry):
         for g in range(groups):
             y_wait(t, g)
+            start = sum(SPANS[:g])
+            first = 0
             if g == 0:
                 x_both(t, "wait_recv")
-            columns = (zero, zero)
-            for x, number in rows_of(g):
-                new = relax(t, g, x, number)
-                for k in range(K):
-                    for h in range(2):
-                        U[t + 1, h, k, x + 1] = new[k][h]
-                    columns = packed(columns, new[k][0], new[k][1], number * K + k)
-                if g == 0 and number == 1:
-                    x_both(t + 1, "start")
-            YO[t + 1, g, 0], YO[t + 1, g, 1] = columns
+                advance(t, 0, 0, 0)
+                advance(t, 0, X - 1, 1)
+                x_both(t + 1, "start")
+                first = 1
+
+            def inwards(n, carry):
+                advance(t, g, start + n, 2 * n)
+                advance(t, g, X - 1 - start - n, 2 * n + 1)
+                return carry
+
+            for n in range(first, SPANS[g]):
+                inwards(n, 0)
+            gather(t + 1, g)
             y_start(t + 1, g)
         sent(t)
         return carry
@@ -324,7 +342,7 @@
 
     def local(fields, source, reaction, velocity, coupling):
         _, _, L, X, Y = fields.shape
-        spans = (2, 6)
+        spans = (3, 5)
         groups = len(spans)
         f32 = jnp.float32
         cells = L * X
@@ -340,7 +358,7 @@
                 pltpu.VMEM((2, K, cells, LANES), f32),
                 pltpu.VMEM((2, K, cells, LANES), f32),
                 pltpu.VMEM((2, 2, cells, LANES), f32),
-                pltpu.VMEM((SWEEPS, 2, K, X + 2, L, LANES), f32),
+                pltpu.VMEM((SWEEPS, X + 2, 2, K, L, LANES), f32),
                 pltpu.VMEM((2, K, X, L, LANES), f32),
                 pltpu.VMEM((2, X, L, LANES), f32),
                 pltpu.VMEM((2, K, X, L, LANES), f32),

time: 33.1 us -> 31.8 us (0.961)
  Pallas kernels: 32.4 us -> 31 us
    pallas_call x1, Pallas kernels: 31.5 us -> 30.1 us  [local(): pl.pallas_call(functools.partial(kernel, nx, ny, L, X, spans), out_shape=...]
where the time goes in v3:
time: 31.8 us; the launch traced here: 31.7 us
  Pallas kernels  31 us (97%)
  between operations  0.64 us (2%)
    pallas_call x1, Pallas kernels, local(): pl.pallas_call(functools.partial(kernel, nx, ny, L, X, spans), out_shape=...  30.1 us
    pallas_call x1, Pallas kernels, local(): pl.pallas_call(write, out_shape=(jax.ShapeDtypeStruct((K, cells, Y), f32)...  0.92 us

profile of v3, /device:TPU:1, one launch (start us, length us, event | category | flops | bytes accessed | tf_op | source)
XLA Modules:
  0.0 31.7 jit_solution(1314999114513992739)
XLA Ops:
  0.6 30.1 %shard_map.68 = (f32[2,3,256,128]{3,2,1,0:T(8,128)S(1)}, f32[2,3,16,128]{3,2,1,0:T(8,128)S(1)}) custom-call(f32[3,256,256]{2,1,0:T(8,128)} %bitcast.7, f32[3,256,256]{2,1,0:T(8,128)} %bitcast.8, f32[256,256]{1,0:T(8,128)} %bitcast.9, f32[256,256]{1,0:T(8,128)} %bitcast.10, f32[3,1,3]{2,1,0:T(1,128)} %bitcast.11), custom_call_target="tpu_custom_call" | custom-call | tf_op jit(solution)/shard_map/pallas_call | solution.py:349
  30.8 0.9 %shard_map.69 = (f32[3,256,256]{2,1,0:T(8,128)}, f32[3,16,256]{2,1,0:T(8,128)}) custom-call(f32[2,3,256,128]{3,2,1,0:T(8,128)S(1)} %get-tuple-element.6.a_ref, f32[2,3,16,128]{3,2,1,0:T(8,128)S(1)} %get-tuple-element.7.b_ref), custom_call_target="tpu_custom_call" | custom-call | tf_op jit(solution)/shard_map/pallas_call | solution.py:396

commit v4 on v2

--- a/solution.py
+++ b/solution.py
@@ -91,15 +91,15 @@
         copy.start()
 
     lane = lax.broadcasted_iota(jnp.int32, (8, LANES), 1)
-    wide_lane = lax.broadcasted_iota(jnp.int32, (L, LANES), 1)
-    row = lax.broadcasted_iota(jnp.int32, (L, LANES), 0)
+    row = lax.broadcasted_iota(jnp.int32, (8, LANES), 0)
+    place = lax.rem(lane + 1, LANES) // 2
     zero = jnp.zeros((8, LANES), jnp.float32)
 
     def x_copy(t, d):
         source, target = ((X, 0), (1, X + 1))[d]
         return pltpu.make_async_remote_copy(
-            U.at[t, :, :, source],
-            U.at[t, :, :, target],
+            U.at[t, source],
+            U.at[t, target],
             xs_sem.at[t, d],
             xr_sem.at[t, d],
             device_id=(east, west)[d],
@@ -108,7 +108,7 @@
 
     def y_copy(t, g, d):
         return pltpu.make_async_remote_copy(
-            YO.at[t, g, d],
+            YO.at[t, g],
             YI.at[t, g, d],
             ys_sem.at[t, g, d],
             yr_sem.at[t, g, d],
@@ -134,22 +134,15 @@
             pl.when(has_north)(lambda: y_copy(t, g, 0).wait_send())
             pl.when(has_south)(lambda: y_copy(t, g, 1).wait_send())
 
-    def packed(columns, first, last, slot):
-        to_north, to_south = columns
-        for part in range(2):
-            place = slot * 2 + part
-            rows = slice(8 * part, 8 * part + 8)
-            to_north = jnp.where(lane == place, pltpu.roll(last[rows], place + 1, 1), to_north)
-            moved = pltpu.roll(first[rows], place, 1) if place else first[rows]
-            to_south = jnp.where(lane == place, moved, to_south)
-        return to_north, to_south
-
-    def unpacked(packet, slot, target):
-        parts = []
-        for part in range(2):
-            shift = (target - (slot * 2 + part)) % LANES
-            parts.append(pltpu.roll(packet, shift, 1) if shift else packet)
-        return jnp.concatenate(parts, axis=0)
+    def packed(packet, first, last, slot):
+        both = jnp.where(lane == LANES - 1, last, first)
+        return jnp.where(place == slot, pltpu.roll(both, 2 * slot, 1) if slot else both, packet)
+
+    def arrived(t, g):
+        return jnp.where(lax.rem(lane, 2) == 0, YI[t, g, 1], pltpu.roll(YI[t, g, 0], 2, 1))
+
+    def slots(number, k):
+        return [(number * K + k) * 2 + part for part in range(2)]
 
     def rows_of(g):
         start = sum(SPANS[:g])
@@ -166,22 +159,16 @@
             M[h, k] = jnp.where(fluid, RATIO * (layer1 - layer0), layer0)
 
     for g in range(groups):
-        columns = (zero, zero)
+        packet = zero
         for x, number in rows_of(g):
             for k in range(K):
-                tiles = []
-                for h in range(2):
-                    tile = jnp.concatenate(
-                        [
-                            F[h, k, pl.ds(8 * part * X + x, 8, stride=X), :]
-                            for part in range(2)
-                        ],
-                        axis=0,
-                    )
-                    U[0, h, k, x + 1] = tile
-                    tiles.append(tile)
-                columns = packed(columns, tiles[0], tiles[1], number * K + k)
-        YO[0, g, 0], YO[0, g, 1] = columns
+                for part, slot in enumerate(slots(number, k)):
+                    rows = pl.ds(8 * part * X + x, 8, stride=X)
+                    tiles = [F[h, k, rows, :] for h in range(2)]
+                    for h in range(2):
+                        U[0, x + 1, h, k, pl.ds(8 * part, 8)] = tiles[h]
+                    packet = packed(packet, tiles[0], tiles[1], slot)
+        YO[0, g] = packet
 
     greeted = 3 + has_south.astype(jnp.int32) + has_north.astype(jnp.int32)
     pl.semaphore_wait(barrier, greeted)
@@ -224,78 +211,92 @@
     ghosts.wait()
     own = jnp.where(fluid, 0.0, 1.0)
 
-    def relax(t, g, x, number):
-        speeds = [V1[h, x] for h in range(2)]
-        center = [[U[t, h, k, x + 1] for h in range(2)] for k in range(K)]
-        new = []
-        for k in range(K):
-            slot = number * K + k
-            from_south = unpacked(YI[t, g, 0], slot, 0)
-            from_north = unpacked(YI[t, g, 1], slot, LANES - 1)
-            up = [pltpu.roll(center[k][h], 1, 1) for h in range(2)]
-            down = [pltpu.roll(center[k][h], LANES - 1, 1) for h in range(2)]
-            souths = (
-                jnp.where(wide_lane == 0, from_south, up[0]),
-                jnp.where(wide_lane == 0, up[0], up[1]),
-            )
-            norths = (
-                jnp.where(wide_lane == LANES - 1, down[1], down[0]),
-                jnp.where(wide_lane == LANES - 1, from_north, down[1]),
-            )
-            results = []
-            for h in range(2):
-                here = center[k][h]
-                ghost = own * here + GH[h, k, pl.ds(x, 1), :]
-                below = jnp.where(row == 0, ghost, pltpu.roll(here, 1, 0))
-                above = jnp.where(row == L - 1, 0.0, pltpu.roll(here, L - 1, 0))
-                total = SS[h, k, x] + below + above
-                total = total + speeds[h] * U[t, h, k, x] + U[t, h, k, x + 2]
-                total = total + souths[h] + norths[h]
-                for j in range(K):
-                    if j != k:
-                        total = total - mix[k][j] * center[j][h]
-                results.append((1.0 - OMEGA) * here + W[h, k, x] * total)
-            new.append(results)
-        return new
+    def relax(t, edges, x, number, parts=(0, 1)):
+        tiles = [pl.ds(8 * part, 8) for part in range(2)]
+
+        def state(x, h, k, part):
+            return U[t, x + 1, h, k, tiles[part]]
+
+        for part in parts:
+            speeds = [V1[h, x, tiles[part]] for h in range(2)]
+            center = [[state(x, h, k, part) for h in range(2)] for k in range(K)]
+            for k in range(K):
+                beyond = pltpu.roll(edges, LANES - 1 - 2 * slots(number, k)[part], 1)
+                up = [pltpu.roll(center[k][h], 1, 1) for h in range(2)]
+                down = [pltpu.roll(center[k][h], LANES - 1, 1) for h in range(2)]
+                souths = (
+                    jnp.where(lane == 0, beyond, up[0]),
+                    jnp.where(lane == 0, up[0], up[1]),
+                )
+                norths = (
+                    jnp.where(lane == LANES - 1, down[1], down[0]),
+                    jnp.where(lane == LANES - 1, beyond, down[1]),
+                )
+                for h in range(2):
+                    here = center[k][h]
+                    beside = state(x, h, k, 1 - part)
+                    if part == 0:
+                        under = own * here + GH[h, k, pl.ds(x, 1), :]
+                        over = pltpu.roll(beside, 7, 0)
+                    else:
+                        under = pltpu.roll(beside, 1, 0)
+                        over = zero
+                    below = jnp.where(row == 0, under, pltpu.roll(here, 1, 0))
+                    above = jnp.where(row == 7, over, pltpu.roll(here, 7, 0))
+                    total = SS[h, k, x, tiles[part]] + below + above
+                    total = total + speeds[h] * state(x - 1, h, k, part) + state(x + 1, h, k, part)
+                    total = total + souths[h] + norths[h]
+                    for j in range(K):
+                        if j != k:
+                            total = total - mix[k][j] * center[j][h]
+                    new = (1.0 - OMEGA) * here + W[h, k, x, tiles[part]] * total
+                    yield k, h, part, new
+
+    def advance(t, edges, x, number):
+        for k, h, part, new in relax(t, edges, x, number):
+            U[t + 1, x + 1, h, k, pl.ds(8 * part, 8)] = new
+
+    def gather(t, g):
+        packet = zero
+        for x, number in rows_of(g):
+            for k in range(K):
+                for part, slot in enumerate(slots(number, k)):
+                    first, last = (U[t, x + 1, h, k, pl.ds(8 * part, 8)] for h in range(2))
+                    packet = packed(packet, first, last, slot)
+        YO[t, g] = packet
 
     def sweep(t, carry):
         for g in range(groups):
             y_wait(t, g)
             if g == 0:
                 x_both(t, "wait_recv")
-            columns = (zero, zero)
+            edges = arrived(t, g)
             for x, number in rows_of(g):
-                new = relax(t, g, x, number)
-                for k in range(K):
-                    for h in range(2):
-                        U[t + 1, h, k, x + 1] = new[k][h]
-                    columns = packed(columns, new[k][0], new[k][1], number * K + k)
+                advance(t, edges, x, number)
                 if g == 0 and number == 1:
                     x_both(t + 1, "start")
-            YO[t + 1, g, 0], YO[t + 1, g, 1] = columns
+            gather(t + 1, g)
             y_start(t + 1, g)
         sent(t)
         return carry
 
     lax.fori_loop(0, SWEEPS - 1, sweep, 0)
 
-    last = SWEEPS - 1
-    for g in range(groups):
-        y_wait(last, g)
-        if g == 0:
-            x_both(last, "wait_recv")
-        for x, number in rows_of(g):
-            new = relax(last, g, x, number)
-            for k in range(K):
-                for h in range(2):
-                    for part in range(2):
-                        rows = pl.ds(8 * part * X + x, 8, stride=X)
-                        O[h, k, rows, :] = new[k][h][8 * part : 8 * part + 8]
-
     traces = pltpu.make_async_remote_copy(
         O.at[:, :, pl.ds(0, X)], PR, p_sem.at[2], p_sem.at[3], device_id=partner, device_id_type=MESH
     )
-    traces.start()
+    last = SWEEPS - 1
+    x_both(last, "wait_recv")
+    for part in range(2):
+        for g in range(groups):
+            if part == 0:
+                y_wait(last, g)
+            edges = arrived(last, g)
+            for x, number in rows_of(g):
+                for k, h, _, new in relax(last, edges, x, number, (part,)):
+                    O[h, k, pl.ds(8 * part * X + x, 8, stride=X), :] = new
+        if part == 0:
+            traces.start()
     sent(last)
     traces.wait()
     mine = jnp.where(fluid, 1.0 - THETA, THETA)
@@ -324,7 +325,7 @@
 
     def local(fields, source, reaction, velocity, coupling):
         _, _, L, X, Y = fields.shape
-        spans = (2, 6)
+        spans = (4, 4)
         groups = len(spans)
         f32 = jnp.float32
         cells = L * X
@@ -340,11 +341,11 @@
                 pltpu.VMEM((2, K, cells, LANES), f32),
                 pltpu.VMEM((2, K, cells, LANES), f32),
                 pltpu.VMEM((2, 2, cells, LANES), f32),
-                pltpu.VMEM((SWEEPS, 2, K, X + 2, L, LANES), f32),
+                pltpu.VMEM((SWEEPS, X + 2, 2, K, L, LANES), f32),
                 pltpu.VMEM((2, K, X, L, LANES), f32),
                 pltpu.VMEM((2, X, L, LANES), f32),
                 pltpu.VMEM((2, K, X, L, LANES), f32),
-                pltpu.VMEM((SWEEPS, groups, 2, 8, LANES), f32),
+                pltpu.VMEM((SWEEPS, groups, 8, LANES), f32),
                 pltpu.VMEM((SWEEPS, groups, 2, 8, LANES), f32),
                 pltpu.VMEM((2, K, X, LANES), f32),
                 pltpu.VMEM((2, K, X, LANES), f32),

time: 33.1 us -> 31.5 us (0.952)
  Pallas kernels: 32.4 us -> 30.7 us
    pallas_call x1, Pallas kernels: 31.5 us -> 29.8 us  [local(): pl.pallas_call(functools.partial(kernel, nx, ny, L, X, spans), out_shape=...]
where the time goes in v4:
time: 31.5 us; the launch traced here: 31.4 us
  Pallas kernels  30.7 us (97%)
  between operations  0.64 us (2%)
    pallas_call x1, Pallas kernels, local(): pl.pallas_call(functools.partial(kernel, nx, ny, L, X, spans), out_shape=...  29.8 us
    pallas_call x1, Pallas kernels, local(): pl.pallas_call(write, out_shape=(jax.ShapeDtypeStruct((K, cells, Y), f32)...  0.92 us

profile of v4, /device:TPU:1, one launch (start us, length us, event | category | flops | bytes accessed | tf_op | source)
XLA Modules:
  0.0 31.4 jit_solution(16140886852572147396)
XLA Ops:
  0.6 29.8 %shard_map.68 = (f32[2,3,256,128]{3,2,1,0:T(8,128)S(1)}, f32[2,3,16,128]{3,2,1,0:T(8,128)S(1)}) custom-call(f32[3,256,256]{2,1,0:T(8,128)} %bitcast.7, f32[3,256,256]{2,1,0:T(8,128)} %bitcast.8, f32[256,256]{1,0:T(8,128)} %bitcast.9, f32[256,256]{1,0:T(8,128)} %bitcast.10, f32[3,1,3]{2,1,0:T(1,128)} %bitcast.11), custom_call_target="tpu_custom_call" | custom-call | tf_op jit(solution)/shard_map/pallas_call | solution.py:332
  30.5 0.9 %shard_map.69 = (f32[3,256,256]{2,1,0:T(8,128)}, f32[3,16,256]{2,1,0:T(8,128)}) custom-call(f32[2,3,256,128]{3,2,1,0:T(8,128)S(1)} %get-tuple-element.6.a_ref, f32[2,3,16,128]{3,2,1,0:T(8,128)S(1)} %get-tuple-element.7.b_ref), custom_call_target="tpu_custom_call" | custom-call | tf_op jit(solution)/shard_map/pallas_call | solution.py:379

commit v5 on v4

v5 whole, which is shorter than its diff:
```python
import functools

import jax
import jax.numpy as jnp
from jax import lax
from jax.experimental import pallas as pl
from jax.experimental.pallas import tpu as pltpu
from jax.sharding import PartitionSpec as P

SWEEPS = 4
K = 3
OMEGA = 0.8
RATIO = 0.5
THETA = 0.7
LANES = 128
MESH = pl.DeviceIdType.MESH


def kernel(
    nx,
    ny,
    L,
    X,
    f_ref,
    s_ref,
    r_ref,
    v_ref,
    c_ref,
    O,
    IO,
    F,
    S,
    RV,
    U,
    W,
    V1,
    SS,
    YO,
    YI,
    M,
    GH,
    PR,
    f_sem,
    s_sem,
    rv_sem,
    xs_sem,
    xr_sem,
    ys_sem,
    yr_sem,
    p_sem,
    C,
    c_sem,
):
    side = lax.axis_index("side")
    gx = lax.axis_index("gx")
    gy = lax.axis_index("gy")
    fluid = side == 0
    west = (side, lax.rem(gx + nx - 1, nx), gy)
    east = (side, lax.rem(gx + 1, nx), gy)
    south = (side, gx, gy - 1)
    north = (side, gx, gy + 1)
    partner = (1 - side, gx, gy)
    has_south = gy > 0
    has_north = gy < ny - 1

    barrier = pltpu.get_barrier_semaphore()

    def greet(device):
        pl.semaphore_signal(barrier, inc=1, device_id=device, device_id_type=MESH)

    greet(west)
    greet(east)
    greet(partner)
    pl.when(has_south)(lambda: greet(south))
    pl.when(has_north)(lambda: greet(north))

    def half(ref, h):
        return ref.at[..., pl.ds(h * LANES, LANES)]

    loads_f = [pltpu.make_async_copy(half(f_ref, h), F.at[h], f_sem.at[h]) for h in range(2)]
    loads_s = [pltpu.make_async_copy(half(s_ref, h), S.at[h], s_sem.at[h]) for h in range(2)]
    loads_rv = [
        pltpu.make_async_copy(half(ref, h), RV.at[n, h], rv_sem.at[n, h])
        for n, ref in enumerate((r_ref, v_ref))
        for h in range(2)
    ]
    load_c = pltpu.make_async_copy(c_ref, C, c_sem)
    for copy in loads_f + loads_rv + loads_s + [load_c]:
        copy.start()

    lane = lax.broadcasted_iota(jnp.int32, (8, LANES), 1)
    row = lax.broadcasted_iota(jnp.int32, (8, LANES), 0)
    zero = jnp.zeros((8, LANES), jnp.float32)

    def x_copy(t, d, h):
        source, target = ((X, 0), (1, X + 1))[d]
        return pltpu.make_async_remote_copy(
            U.at[t, source, h],
            U.at[t, target, h],
            xs_sem.at[t, d, h],
            xr_sem.at[t, d, h],
            device_id=(east, west)[d],
            device_id_type=MESH,
        )

    def y_copy(t, g, d):
        return pltpu.make_async_remote_copy(
            YO.at[t, g, d],
            YI.at[t, g, d],
            ys_sem.at[t, g, d],
            yr_sem.at[t, g, d],
            device_id=(north, south)[d],
            device_id_type=MESH,
        )

    quarters = [(g, h) for g in range(2) for h in range(2)]

    def y_start(t, g, h):
        pl.when((has_south, has_north)[h])(lambda: y_copy(t, g, 1 - h).start())

    def y_sent(t, g, h):
        pl.when((has_south, has_north)[h])(lambda: y_copy(t, g, 1 - h).wait_send())

    def arrive(t, g, h):
        pl.when((has_south, has_north)[h])(lambda: y_copy(t, g, h).wait_recv())
        x_copy(t, 1 - g, h).wait_recv()

    def sent(t):
        for g, h in quarters:
            x_copy(t, g, h).wait_send()
            y_sent(t, g, h)

    def packed(packet, tile, h, slot):
        shift = slot + h
        moved = pltpu.roll(tile, shift, 1) if shift else tile
        return jnp.where(lane == slot, moved, packet)

    def unpacked(packet, h, slot):
        shift = (h * (LANES - 1) - slot) % LANES
        return pltpu.roll(packet, shift, 1) if shift else packet

    def slots(number, k):
        return [(number * K + k) * 2 + part for part in range(2)]

    def rows_of(g):
        return [(n if g else X - 1 - n, n) for n in range(X // 2)]

    for copy in loads_f:
        copy.wait()

    for h in range(2):
        for k in range(K):
            layer0, layer1 = F[h, k, 0:X], F[h, k, X : 2 * X]
            M[h, k] = jnp.where(fluid, RATIO * (layer1 - layer0), layer0)

    for g, h in quarters:
        packet = zero
        for x, number in rows_of(g):
            for k in range(K):
                for part, slot in enumerate(slots(number, k)):
                    tile = F[h, k, pl.ds(8 * part * X + x, 8, stride=X), :]
                    U[0, x + 1, h, k, pl.ds(8 * part, 8)] = tile
                    packet = packed(packet, tile, h, slot)
        YO[0, g, 1 - h] = packet

    greeted = 3 + has_south.astype(jnp.int32) + has_north.astype(jnp.int32)
    pl.semaphore_wait(barrier, greeted)

    for g, h in quarters:
        y_start(0, g, h)
    for g, h in quarters:
        x_copy(0, g, h).start()
    ghosts = pltpu.make_async_remote_copy(
        M, GH, p_sem.at[0], p_sem.at[1], device_id=partner, device_id_type=MESH
    )
    ghosts.start()

    def blank(d):
        for t in range(SWEEPS):
            for g in range(2):
                YI[t, g, d] = zero

    pl.when(jnp.logical_not(has_south))(lambda: blank(0))
    pl.when(jnp.logical_not(has_north))(lambda: blank(1))

    for copy in loads_rv + loads_s + [load_c]:
        copy.wait()
    mix = [[C[k, 0, j] for j in range(K)] for k in range(K)]

    def weigh(x, carry):
        for h in range(2):
            for part in range(2):
                rows = pl.ds(8 * part * X + x, 8, stride=X)
                out = pl.ds(8 * part, 8)
                speed = RV[1, h, rows, :]
                diag = 6.0 + RV[0, h, rows, :] + speed
                V1[h, x, out] = 1.0 + speed
                for k in range(K):
                    W[h, k, x, out] = OMEGA / (diag + mix[k][k])
                    SS[h, k, x, out] = S[h, k, rows, :]
        return carry

    lax.fori_loop(0, X, weigh, 0)

    ghosts.wait()
    own = jnp.where(fluid, 0.0, 1.0)

    def relax(t, packet, x, number, h, parts=(0, 1)):
        tiles = [pl.ds(8 * part, 8) for part in range(2)]
        outer, inner = ((0, LANES - 1), (LANES - 1, 0))[h]
        away, back = ((1, LANES - 1), (LANES - 1, 1))[h]

        def state(x, h, k, part):
            return U[t, x + 1, h, k, tiles[part]]

        for part in parts:
            speed = V1[h, x, tiles[part]]
            center = [state(x, h, k, part) for k in range(K)]
            for k in range(K):
                here = center[k]
                beyond = unpacked(packet, h, slots(number, k)[part])
                outwards = jnp.where(lane == outer, beyond, pltpu.roll(here, away, 1))
                across = jnp.where(lane == outer, state(x, 1 - h, k, part), here)
                inwards = pltpu.roll(across, back, 1)
                beside = state(x, h, k, 1 - part)
                if part == 0:
                    under = own * here + GH[h, k, pl.ds(x, 1), :]
                    over = pltpu.roll(beside, 7, 0)
                else:
                    under = pltpu.roll(beside, 1, 0)
                    over = zero
                below = jnp.where(row == 0, under, pltpu.roll(here, 1, 0))
                above = jnp.where(row == 7, over, pltpu.roll(here, 7, 0))
                total = SS[h, k, x, tiles[part]] + below + above
                total = total + speed * state(x - 1, h, k, part) + state(x + 1, h, k, part)
                total = total + outwards + inwards
                for j in range(K):
                    if j != k:
                        total = total - mix[k][j] * center[j]
                yield k, part, (1.0 - OMEGA) * here + W[h, k, x, tiles[part]] * total

    def gather(t, g, h):
        packet = zero
        for x, number in rows_of(g):
            for k in range(K):
                for part, slot in enumerate(slots(number, k)):
                    packet = packed(packet, U[t, x + 1, h, k, pl.ds(8 * part, 8)], h, slot)
        YO[t, g, 1 - h] = packet

    def sweep(t, carry):
        for g, h in quarters:
            arrive(t, g, h)
            packet = YI[t, g, h]
            for x, number in rows_of(g):
                for k, part, new in relax(t, packet, x, number, h):
                    U[t + 1, x + 1, h, k, pl.ds(8 * part, 8)] = new
                if number == 0:
                    x_copy(t + 1, g, h).start()
            gather(t + 1, g, h)
            y_start(t + 1, g, h)
        sent(t)
        return carry

    lax.fori_loop(0, SWEEPS - 1, sweep, 0)

    traces = pltpu.make_async_remote_copy(
        O.at[:, :, pl.ds(0, X)], PR, p_sem.at[2], p_sem.at[3], device_id=partner, device_id_type=MESH
    )
    last = SWEEPS - 1
    for part in range(2):
        for g, h in quarters:
            if part == 0:
                arrive(last, g, h)
            packet = YI[last, g, h]
            for x, number in rows_of(g):
                for k, _, new in relax(last, packet, x, number, h, (part,)):
                    O[h, k, pl.ds(8 * part * X + x, 8, stride=X), :] = new
        if part == 0:
            traces.start()
    sent(last)
    traces.wait()
    mine = jnp.where(fluid, 1.0 - THETA, THETA)
    other = jnp.where(fluid, THETA, 1.0 - THETA)
    for h in range(2):
        for k in range(K):
            IO[h, k] = mine * O[h, k, 0:X] + other * PR[h, k]


def write(a_ref, b_ref, o_ref, i_ref, sem):
    copies = [
        pltpu.make_async_copy(
            tile_ref.at[h], out_ref.at[..., pl.ds(h * LANES, LANES)], sem.at[n, h]
        )
        for n, (tile_ref, out_ref) in enumerate(((a_ref, o_ref), (b_ref, i_ref)))
        for h in range(2)
    ]
    for copy in copies:
        copy.start()
    for copy in copies:
        copy.wait()


def solution(mesh):
    nx, ny = mesh.shape["gx"], mesh.shape["gy"]

    def local(fields, source, reaction, velocity, coupling):
        _, _, L, X, Y = fields.shape
        groups = 2
        f32 = jnp.float32
        cells = L * X
        tiles, edges = pl.pallas_call(
            functools.partial(kernel, nx, ny, L, X),
            out_shape=(
                pltpu.VMEM((2, K, cells, LANES), f32),
                pltpu.VMEM((2, K, X, LANES), f32),
            ),
            in_specs=[pl.BlockSpec(memory_space=pltpu.HBM)] * 5,
            out_specs=[pl.BlockSpec(memory_space=pltpu.VMEM)] * 2,
            scratch_shapes=[
                pltpu.VMEM((2, K, cells, LANES), f32),
                pltpu.VMEM((2, K, cells, LANES), f32),
                pltpu.VMEM((2, 2, cells, LANES), f32),
                pltpu.VMEM((SWEEPS, X + 2, 2, K, L, LANES), f32),
                pltpu.VMEM((2, K, X, L, LANES), f32),
                pltpu.VMEM((2, X, L, LANES), f32),
                pltpu.VMEM((2, K, X, L, LANES), f32),
                pltpu.VMEM((SWEEPS, groups, 2, 8, LANES), f32),
                pltpu.VMEM((SWEEPS, groups, 2, 8, LANES), f32),
                pltpu.VMEM((2, K, X, LANES), f32),
                pltpu.VMEM((2, K, X, LANES), f32),
                pltpu.VMEM((2, K, X, LANES), f32),
                pltpu.SemaphoreType.DMA((2,)),
                pltpu.SemaphoreType.DMA((2,)),
                pltpu.SemaphoreType.DMA((2, 2)),
                pltpu.SemaphoreType.DMA((SWEEPS, 2, 2)),
                pltpu.SemaphoreType.DMA((SWEEPS, 2, 2)),
                pltpu.SemaphoreType.DMA((SWEEPS, groups, 2)),
                pltpu.SemaphoreType.DMA((SWEEPS, groups, 2)),
                pltpu.SemaphoreType.DMA((4,)),
                pltpu.SMEM((K, 1, K), f32),
                pltpu.SemaphoreType.DMA,
            ],
            compiler_params=pltpu.CompilerParams(
                collective_id=0,
                has_side_effects=True,
                vmem_limit_bytes=60 * 1024 * 1024,
            ),
        )(
            fields.reshape(K, cells, Y),
            source.reshape(K, cells, Y),
            reaction.reshape(cells, Y),
            velocity.reshape(cells, Y),
            coupling.reshape(K, 1, K),
        )
        tiles, edges = (
            pltpu.with_memory_space_constraint(value, pltpu.VMEM) for value in (tiles, edges)
        )
        new, interface = pl.pallas_call(
            write,
            out_shape=(
                jax.ShapeDtypeStruct((K, cells, Y), f32),
                jax.ShapeDtypeStruct((K, X, Y), f32),
            ),
            in_specs=[pl.BlockSpec(memory_space=pltpu.VMEM)] * 2,
            out_specs=[pl.BlockSpec(memory_space=pltpu.HBM)] * 2,
            scratch_shapes=[pltpu.SemaphoreType.DMA((2, 2))],
        )(tiles, edges)
        return new.reshape(1, K, L, X, Y), interface[None]

    return jax.shard_map(
        local,
        mesh=mesh,
        in_specs=(
            P("side", None, None, "gx", "gy"),
            P("side", None, None, "gx", "gy"),
            P("side", None, "gx", "gy"),
            P("side", None, "gx", "gy"),
            P("side", None, None),
        ),
        out_specs=(P("side", None, None, "gx", "gy"), P("side", None, "gx", "gy")),
        check_vma=False,
    )
```

time: 31.5 us -> 29.6 us (0.940)
  Pallas kernels: 30.7 us -> 28.8 us
    pallas_call x1, Pallas kernels: 29.8 us -> 27.9 us  [local(): pl.pallas_call(functools.partial(kernel, nx, ny, L, X), out_shape=(pltpu....]
where the time goes in v5:
time: 29.6 us; the launch traced here: 29.5 us
  Pallas kernels  28.8 us (97%)
  between operations  0.64 us (2%)
    pallas_call x1, Pallas kernels, local(): pl.pallas_call(functools.partial(kernel, nx, ny, L, X), out_shape=(pltpu....  27.9 us
    pallas_call x1, Pallas kernels, local(): pl.pallas_call(write, out_shape=(jax.ShapeDtypeStruct((K, cells, Y), f32)...  0.92 us

profile of v5, /device:TPU:1, one launch (start us, length us, event | category | flops | bytes accessed | tf_op | source)
XLA Modules:
  0.0 29.5 jit_solution(10414818344634085346)
XLA Ops:
  0.6 27.9 %shard_map.68 = (f32[2,3,256,128]{3,2,1,0:T(8,128)S(1)}, f32[2,3,16,128]{3,2,1,0:T(8,128)S(1)}) custom-call(f32[3,256,256]{2,1,0:T(8,128)} %bitcast.7, f32[3,256,256]{2,1,0:T(8,128)} %bitcast.8, f32[256,256]{1,0:T(8,128)} %bitcast.9, f32[256,256]{1,0:T(8,128)} %bitcast.10, f32[3,1,3]{2,1,0:T(1,128)} %bitcast.11), custom_call_target="tpu_custom_call" | custom-call | tf_op jit(solution)/shard_map/pallas_call | solution.py:311
  28.5 0.9 %shard_map.69 = (f32[3,256,256]{2,1,0:T(8,128)}, f32[3,16,256]{2,1,0:T(8,128)}) custom-call(f32[2,3,256,128]{3,2,1,0:T(8,128)S(1)} %get-tuple-element.6.a_ref, f32[2,3,16,128]{3,2,1,0:T(8,128)S(1)} %get-tuple-element.7.b_ref), custom_call_target="tpu_custom_call" | custom-call | tf_op jit(solution)/shard_map/pallas_call | solution.py:358

commit v6 on v5

--- a/solution.py
+++ b/solution.py
@@ -48,6 +48,8 @@
     ys_sem,
     yr_sem,
     p_sem,
+    ts_sem,
+    tr_sem,
     C,
     c_sem,
 ):
@@ -89,14 +91,13 @@
         copy.start()
 
     lane = lax.broadcasted_iota(jnp.int32, (8, LANES), 1)
-    row = lax.broadcasted_iota(jnp.int32, (8, LANES), 0)
     zero = jnp.zeros((8, LANES), jnp.float32)
 
     def x_copy(t, d, h):
         source, target = ((X, 0), (1, X + 1))[d]
         return pltpu.make_async_remote_copy(
-            U.at[t, source, h],
-            U.at[t, target, h],
+            U.at[t, source, h, :, pl.ds(8, L)],
+            U.at[t, target, h, :, pl.ds(8, L)],
             xs_sem.at[t, d, h],
             xr_sem.at[t, d, h],
             device_id=(east, west)[d],
@@ -159,7 +160,7 @@
             for k in range(K):
                 for part, slot in enumerate(slots(number, k)):
                     tile = F[h, k, pl.ds(8 * part * X + x, 8, stride=X), :]
-                    U[0, x + 1, h, k, pl.ds(8 * part, 8)] = tile
+                    U[0, x + 1, h, k, pl.ds(8 + 8 * part, 8)] = tile
                     packet = packed(packet, tile, h, slot)
         YO[0, g, 1 - h] = packet
 
@@ -205,13 +206,26 @@
     ghosts.wait()
     own = jnp.where(fluid, 0.0, 1.0)
 
+    def ghost(h, k, x, layer):
+        return own * layer + GH[h, k, pl.ds(x, 1), :]
+
+    def frame(x, carry):
+        for h in range(2):
+            for k in range(K):
+                for t in range(SWEEPS):
+                    U[t, x + 1, h, k, pl.ds(8 + L, 8)] = zero
+                U[0, x + 1, h, k, 7:8] = ghost(h, k, x, U[0, x + 1, h, k, 8:9])
+        return carry
+
+    lax.fori_loop(0, X, frame, 0)
+
     def relax(t, packet, x, number, h, parts=(0, 1)):
         tiles = [pl.ds(8 * part, 8) for part in range(2)]
         outer, inner = ((0, LANES - 1), (LANES - 1, 0))[h]
         away, back = ((1, LANES - 1), (LANES - 1, 1))[h]
 
-        def state(x, h, k, part):
-            return U[t, x + 1, h, k, tiles[part]]
+        def state(x, h, k, part, up=0):
+            return U[t, x + 1, h, k, pl.ds(8 + 8 * part + up, 8)]
 
         for part in parts:
             speed = V1[h, x, tiles[part]]
@@ -222,16 +236,7 @@
                 outwards = jnp.where(lane == outer, beyond, pltpu.roll(here, away, 1))
                 across = jnp.where(lane == outer, state(x, 1 - h, k, part), here)
                 inwards = pltpu.roll(across, back, 1)
-                beside = state(x, h, k, 1 - part)
-                if part == 0:
-                    under = own * here + GH[h, k, pl.ds(x, 1), :]
-                    over = pltpu.roll(beside, 7, 0)
-                else:
-                    under = pltpu.roll(beside, 1, 0)
-                    over = zero
-                below = jnp.where(row == 0, under, pltpu.roll(here, 1, 0))
-                above = jnp.where(row == 7, over, pltpu.roll(here, 7, 0))
-                total = SS[h, k, x, tiles[part]] + below + above
+                total = SS[h, k, x, tiles[part]] + state(x, h, k, part, -1) + state(x, h, k, part, 1)
                 total = total + speed * state(x - 1, h, k, part) + state(x + 1, h, k, part)
                 total = total + outwards + inwards
                 for j in range(K):
@@ -244,7 +249,7 @@
         for x, number in rows_of(g):
             for k in range(K):
                 for part, slot in enumerate(slots(number, k)):
-                    packet = packed(packet, U[t, x + 1, h, k, pl.ds(8 * part, 8)], h, slot)
+                    packet = packed(packet, U[t, x + 1, h, k, pl.ds(8 + 8 * part, 8)], h, slot)
         YO[t, g, 1 - h] = packet
 
     def sweep(t, carry):
@@ -253,37 +258,48 @@
             packet = YI[t, g, h]
             for x, number in rows_of(g):
                 for k, part, new in relax(t, packet, x, number, h):
-                    U[t + 1, x + 1, h, k, pl.ds(8 * part, 8)] = new
-                if number == 0:
-                    x_copy(t + 1, g, h).start()
+                    U[t + 1, x + 1, h, k, pl.ds(8 + 8 * part, 8)] = new
+                    if part == 0:
+                        U[t + 1, x + 1, h, k, 7:8] = ghost(h, k, x, new[0:1])
             gather(t + 1, g, h)
             y_start(t + 1, g, h)
+            x_copy(t + 1, g, h).start()
         sent(t)
         return carry
 
     lax.fori_loop(0, SWEEPS - 1, sweep, 0)
 
-    traces = pltpu.make_async_remote_copy(
-        O.at[:, :, pl.ds(0, X)], PR, p_sem.at[2], p_sem.at[3], device_id=partner, device_id_type=MESH
-    )
     last = SWEEPS - 1
-    for part in range(2):
-        for g, h in quarters:
-            if part == 0:
-                arrive(last, g, h)
-            packet = YI[last, g, h]
+    half_rows = X // 2
+
+    def trace(g, h):
+        rows = pl.ds((1 - g) * half_rows, half_rows)
+        return pltpu.make_async_remote_copy(
+            O.at[h, :, rows],
+            PR.at[h, :, rows],
+            ts_sem.at[g, h],
+            tr_sem.at[g, h],
+            device_id=partner,
+            device_id_type=MESH,
+        )
+
+    for g, h in quarters:
+        arrive(last, g, h)
+        packet = YI[last, g, h]
+        for part in range(2):
             for x, number in rows_of(g):
                 for k, _, new in relax(last, packet, x, number, h, (part,)):
                     O[h, k, pl.ds(8 * part * X + x, 8, stride=X), :] = new
-        if part == 0:
-            traces.start()
+            if part == 0:
+                trace(g, h).start()
     sent(last)
-    traces.wait()
     mine = jnp.where(fluid, 1.0 - THETA, THETA)
     other = jnp.where(fluid, THETA, 1.0 - THETA)
-    for h in range(2):
+    for g, h in quarters:
+        trace(g, h).wait()
+        rows = pl.ds((1 - g) * half_rows, half_rows)
         for k in range(K):
-            IO[h, k] = mine * O[h, k, 0:X] + other * PR[h, k]
+            IO[h, k, rows] = mine * O[h, k, rows] + other * PR[h, k, rows]
 
 
 def write(a_ref, b_ref, o_ref, i_ref, sem):
@@ -320,7 +336,7 @@
                 pltpu.VMEM((2, K, cells, LANES), f32),
                 pltpu.VMEM((2, K, cells, LANES), f32),
                 pltpu.VMEM((2, 2, cells, LANES), f32),
-                pltpu.VMEM((SWEEPS, X + 2, 2, K, L, LANES), f32),
+                pltpu.VMEM((SWEEPS, X + 2, 2, K, L + 16, LANES), f32),
                 pltpu.VMEM((2, K, X, L, LANES), f32),
                 pltpu.VMEM((2, X, L, LANES), f32),
                 pltpu.VMEM((2, K, X, L, LANES), f32),
@@ -336,7 +352,9 @@
                 pltpu.SemaphoreType.DMA((SWEEPS, 2, 2)),
                 pltpu.SemaphoreType.DMA((SWEEPS, groups, 2)),
                 pltpu.SemaphoreType.DMA((SWEEPS, groups, 2)),
-                pltpu.SemaphoreType.DMA((4,)),
+                pltpu.SemaphoreType.DMA((2,)),
+                pltpu.SemaphoreType.DMA((2, 2)),
+                pltpu.SemaphoreType.DMA((2, 2)),
                 pltpu.SMEM((K, 1, K), f32),
                 pltpu.SemaphoreType.DMA,
             ],

time: 29.6 us -> 29.1 us (0.983)
  Pallas kernels: 28.8 us -> 28.3 us
    pallas_call x1, Pallas kernels: 27.9 us -> 27.4 us  [local(): pl.pallas_call(functools.partial(kernel, nx, ny, L, X), out_shape=(pltpu....]
where the time goes in v6:
time: 29.1 us; the launch traced here: 29 us
  Pallas kernels  28.3 us (97%)
  between operations  0.64 us (2%)
    pallas_call x1, Pallas kernels, local(): pl.pallas_call(functools.partial(kernel, nx, ny, L, X), out_shape=(pltpu....  27.4 us
    pallas_call x1, Pallas kernels, local(): pl.pallas_call(write, out_shape=(jax.ShapeDtypeStruct((K, cells, Y), f32)...  0.92 us

profile of v6, /device:TPU:1, one launch (start us, length us, event | category | flops | bytes accessed | tf_op | source)
XLA Modules:
  0.0 29.0 jit_solution(9246106924836095720)
XLA Ops:
  0.6 27.4 %shard_map.68 = (f32[2,3,256,128]{3,2,1,0:T(8,128)S(1)}, f32[2,3,16,128]{3,2,1,0:T(8,128)S(1)}) custom-call(f32[3,256,256]{2,1,0:T(8,128)} %bitcast.7, f32[3,256,256]{2,1,0:T(8,128)} %bitcast.8, f32[256,256]{1,0:T(8,128)} %bitcast.9, f32[256,256]{1,0:T(8,128)} %bitcast.10, f32[3,1,3]{2,1,0:T(1,128)} %bitcast.11), custom_call_target="tpu_custom_call" | custom-call | tf_op jit(solution)/shard_map/pallas_call | solution.py:327
  28.0 0.9 %shard_map.69 = (f32[3,256,256]{2,1,0:T(8,128)}, f32[3,16,256]{2,1,0:T(8,128)}) custom-call(f32[2,3,256,128]{3,2,1,0:T(8,128)S(1)} %get-tuple-element.6.a_ref, f32[2,3,16,128]{3,2,1,0:T(8,128)S(1)} %get-tuple-element.7.b_ref), custom_call_target="tpu_custom_call" | custom-call | tf_op jit(solution)/shard_map/pallas_call | solution.py:376

commit v7 on v6

--- a/solution.py
+++ b/solution.py
@@ -52,6 +52,7 @@
     tr_sem,
     C,
     c_sem,
+    WP,
 ):
     side = lax.axis_index("side")
     gx = lax.axis_index("gx")
@@ -122,9 +123,8 @@
     def y_sent(t, g, h):
         pl.when((has_south, has_north)[h])(lambda: y_copy(t, g, 1 - h).wait_send())
 
-    def arrive(t, g, h):
+    def y_wait(t, g, h):
         pl.when((has_south, has_north)[h])(lambda: y_copy(t, g, h).wait_recv())
-        x_copy(t, 1 - g, h).wait_recv()
 
     def sent(t):
         for g, h in quarters:
@@ -219,7 +219,19 @@
 
     lax.fori_loop(0, X, frame, 0)
 
-    def relax(t, packet, x, number, h, parts=(0, 1)):
+    for g, h in quarters:
+        weights = zero
+        for x, number in rows_of(g):
+            for k in range(K):
+                for part, slot in enumerate(slots(number, k)):
+                    weights = packed(weights, W[h, k, x, pl.ds(8 * part, 8)], h, slot)
+        WP[g, h] = weights
+
+    def share(packet, x, number, h, k, part):
+        beyond = unpacked(packet, h, slots(number, k)[part])
+        return jnp.where(lane == h * (LANES - 1), W[h, k, x, pl.ds(8 * part, 8)] * beyond, 0.0)
+
+    def relax(t, x, h):
         tiles = [pl.ds(8 * part, 8) for part in range(2)]
         outer, inner = ((0, LANES - 1), (LANES - 1, 0))[h]
         away, back = ((1, LANES - 1), (LANES - 1, 1))[h]
@@ -227,13 +239,12 @@
         def state(x, h, k, part, up=0):
             return U[t, x + 1, h, k, pl.ds(8 + 8 * part + up, 8)]
 
-        for part in parts:
+        for part in range(2):
             speed = V1[h, x, tiles[part]]
             center = [state(x, h, k, part) for k in range(K)]
             for k in range(K):
                 here = center[k]
-                beyond = unpacked(packet, h, slots(number, k)[part])
-                outwards = jnp.where(lane == outer, beyond, pltpu.roll(here, away, 1))
+                outwards = jnp.where(lane == outer, 0.0, pltpu.roll(here, away, 1))
                 across = jnp.where(lane == outer, state(x, 1 - h, k, part), here)
                 inwards = pltpu.roll(across, back, 1)
                 total = SS[h, k, x, tiles[part]] + state(x, h, k, part, -1) + state(x, h, k, part, 1)
@@ -244,26 +255,44 @@
                         total = total - mix[k][j] * center[j]
                 yield k, part, (1.0 - OMEGA) * here + W[h, k, x, tiles[part]] * total
 
-    def gather(t, g, h):
-        packet = zero
-        for x, number in rows_of(g):
+    def gather(t, h, rows, packet):
+        for x, number in rows:
             for k in range(K):
                 for part, slot in enumerate(slots(number, k)):
                     packet = packed(packet, U[t, x + 1, h, k, pl.ds(8 + 8 * part, 8)], h, slot)
-        YO[t, g, 1 - h] = packet
+        return packet
+
+    def advance(t, x, h):
+        for k, part, new in relax(t, x, h):
+            U[t + 1, x + 1, h, k, pl.ds(8 + 8 * part, 8)] = new
+            if part == 0:
+                U[t + 1, x + 1, h, k, 7:8] = ghost(h, k, x, new[0:1])
 
     def sweep(t, carry):
+        packets = {}
         for g, h in quarters:
-            arrive(t, g, h)
-            packet = YI[t, g, h]
+            inner = rows_of(g)[1:]
+            for x, _ in inner:
+                advance(t, x, h)
+            packets[g, h] = gather(t + 1, h, inner, zero)
+        for g, h in quarters:
+            edge = rows_of(g)[:1]
+            x_copy(t, 1 - g, h).wait_recv()
+            advance(t, edge[0][0], h)
+            packet = gather(t + 1, h, edge, packets[g, h])
+            y_wait(t, g, h)
+            beyond = YI[t, g, h]
+            YO[t + 1, g, 1 - h] = packet + WP[g, h] * beyond
+            y_start(t + 1, g, h)
             for x, number in rows_of(g):
-                for k, part, new in relax(t, packet, x, number, h):
-                    U[t + 1, x + 1, h, k, pl.ds(8 + 8 * part, 8)] = new
-                    if part == 0:
-                        U[t + 1, x + 1, h, k, 7:8] = ghost(h, k, x, new[0:1])
-            gather(t + 1, g, h)
-            y_start(t + 1, g, h)
-            x_copy(t + 1, g, h).start()
+                for k in range(K):
+                    for part in range(2):
+                        more = share(beyond, x, number, h, k, part)
+                        U[t + 1, x + 1, h, k, pl.ds(8 + 8 * part, 8)] += more
+                        if part == 0:
+                            U[t + 1, x + 1, h, k, 7:8] += own * more[0:1]
+                if number == 0:
+                    x_copy(t + 1, g, h).start()
         sent(t)
         return carry
 
@@ -283,13 +312,23 @@
             device_id_type=MESH,
         )
 
-    for g, h in quarters:
-        arrive(last, g, h)
-        packet = YI[last, g, h]
+    def conclude(x, h):
+        for k, part, new in relax(last, x, h):
+            O[h, k, pl.ds(8 * part * X + x, 8, stride=X), :] = new
+
+    for g, h in quarters:
+        for x, _ in rows_of(g)[1:]:
+            conclude(x, h)
+    for g, h in quarters:
+        x_copy(last, 1 - g, h).wait_recv()
+        conclude(rows_of(g)[0][0], h)
+        y_wait(last, g, h)
+        beyond = YI[last, g, h]
         for part in range(2):
             for x, number in rows_of(g):
-                for k, _, new in relax(last, packet, x, number, h, (part,)):
-                    O[h, k, pl.ds(8 * part * X + x, 8, stride=X), :] = new
+                for k in range(K):
+                    rows = pl.ds(8 * part * X + x, 8, stride=X)
+                    O[h, k, rows, :] += share(beyond, x, number, h, k, part)
             if part == 0:
                 trace(g, h).start()
     sent(last)
@@ -357,6 +396,7 @@
                 pltpu.SemaphoreType.DMA((2, 2)),
                 pltpu.SMEM((K, 1, K), f32),
                 pltpu.SemaphoreType.DMA,
+                pltpu.VMEM((2, 2, 8, LANES), f32),
             ],
             compiler_params=pltpu.CompilerParams(
                 collective_id=0,

time: 29.1 us -> 28.7 us (0.986)
  Pallas kernels: 28.3 us -> 28 us
    pallas_call x1, Pallas kernels: 27.4 us -> 27 us  [local(): pl.pallas_call(functools.partial(kernel, nx, ny, L, X), out_shape=(pltpu....]
where the time goes in v7:
time: 28.7 us; the launch traced here: 28.6 us
  Pallas kernels  28 us (98%)
  between operations  0.64 us (2%)
    pallas_call x1, Pallas kernels, local(): pl.pallas_call(functools.partial(kernel, nx, ny, L, X), out_shape=(pltpu....  27 us
    pallas_call x1, Pallas kernels, local(): pl.pallas_call(write, out_shape=(jax.ShapeDtypeStruct((K, cells, Y), f32)...  0.92 us

profile of v7, /device:TPU:1, one launch (start us, length us, event | category | flops | bytes accessed | tf_op | source)
XLA Modules:
  0.0 28.6 jit_solution(10892442131321263480)
XLA Ops:
  0.6 27.0 %shard_map.68 = (f32[2,3,256,128]{3,2,1,0:T(8,128)S(1)}, f32[2,3,16,128]{3,2,1,0:T(8,128)S(1)}) custom-call(f32[3,256,256]{2,1,0:T(8,128)} %bitcast.7, f32[3,256,256]{2,1,0:T(8,128)} %bitcast.8, f32[256,256]{1,0:T(8,128)} %bitcast.9, f32[256,256]{1,0:T(8,128)} %bitcast.10, f32[3,1,3]{2,1,0:T(1,128)} %bitcast.11), custom_call_target="tpu_custom_call" | custom-call | tf_op jit(solution)/shard_map/pallas_call | solution.py:366
  27.7 0.9 %shard_map.69 = (f32[3,256,256]{2,1,0:T(8,128)}, f32[3,16,256]{2,1,0:T(8,128)}) custom-call(f32[2,3,256,128]{3,2,1,0:T(8,128)S(1)} %get-tuple-element.6.a_ref, f32[2,3,16,128]{3,2,1,0:T(8,128)S(1)} %get-tuple-element.7.b_ref), custom_call_target="tpu_custom_call" | custom-call | tf_op jit(solution)/shard_map/pallas_call | solution.py:416
